TPU v7x, 32 devices: a whole 2x2x4 slice. The times are simulated.
32 devices in a mesh: band: 4 (over y, x), tile: 8 (over z, core).
Axes of the slice: x: 2, y: 2, z: 4, core: 2. Of those that a mesh axis runs over, the one named last changes fastest.
Arguments:
- granules: bfloat16 [128, 16, 4096], P('tile', 'band'), may hold values from -6 to 6
- valid_rows: int32 [128, 64], P('tile'), may hold values 0 or 1
- scene_order: int32 [128], P('tile'), may hold values from 0 to 127, each once
- intersections: int32 [128, 4], P('tile'), may hold values from 0 to 7, all different within a row; in each aligned block of 16 rows (0 to 15, 16 to 31, ...) at most 9 rows name the same one
- row_resample: bfloat16 [128, 4, 4096], P('tile'), may hold values from 0 to 1.4, as said below
- col_resample: bfloat16 [128, 4, 4096], P('tile'), may hold values from 0 to 1.4, as said below
- w_in: bfloat16 [16, 256], replicated, may hold values from -1.5 to 1.5
- w_hidden: bfloat16 [2, 256, 256], replicated, may hold values from -0.375 to 0.375
- w_out: bfloat16 [256], replicated, may hold values from -1.5 to 1.5
Outputs:
- composite: float32 [16, 32768], P('band', 'tile')
Inputs may be any that keep to these rules, and one draw needn't show every extreme that they name: `intersections`: each scene names 4 different output tiles; the 16 scenes of one device name any one tile at most 9 times, a bound that some block reaches. `scene_order`: each order number appears once. `row_resample`: nonnegative resampling weights. `col_resample`: nonnegative resampling weights.
All inputs are finite; a program needn't handle non-finite values. No bound on the sum of `valid_rows` on one device may be relied on, other than what follows from the above.
Results may differ from a plain program's by a relative error of at most 0.0031.
Values may be sent and summed in bfloat16 or wider, within the bound.
A program may use at most 128 MiB of HBM per device.

v0:
```python
import jax
import jax.numpy as jnp
from jax import lax
from jax.sharding import PartitionSpec as P

HUBER_ITERS = 4
SMOOTH = 2


prior_weight = 0.25
huber_delta = 0.5
edge_scale = 1.0
smooth_rate = 0.2


def extended_2(block, sides, width):
    for axis, dim in sides:
        count = lax.axis_size(axis)
        forward = [(i, i + 1) for i in range(count - 1)]
        backward = [(target, source) for source, target in forward]
        low = lax.ppermute(
            lax.slice_in_dim(block, block.shape[dim] - width, None, axis=dim), axis, forward
        )
        high = lax.ppermute(lax.slice_in_dim(block, 0, width, axis=dim), axis, backward)
        block = jnp.concatenate([low, block, high], axis=dim)
    return block


def scene_weights(pixels, valid_part, recency, w_in, w_hidden, w_out, side_cells):
    scenes, row_count = valid_part.shape
    valid_pix = jnp.broadcast_to(
        valid_part.astype(jnp.float32)[:, :, None], (scenes, row_count, side_cells)
    )
    valid_pix = valid_pix.reshape(scenes, row_count * side_cells)

    def one_scene(inputs):
        scene_pixels, scene_valid, scene_recency = inputs
        hidden = jax.nn.silu(
            jnp.einsum("cn,ch->nh", scene_pixels, w_in, preferred_element_type=jnp.float32)
        ).astype(jnp.bfloat16)
        for repeat in range(w_hidden.shape[0]):
            hidden = jax.nn.silu(
                jnp.dot(hidden, w_hidden[repeat], preferred_element_type=jnp.float32)
            ).astype(jnp.bfloat16)
        logits = jnp.dot(hidden, w_out, preferred_element_type=jnp.float32)
        return (jax.nn.sigmoid(-logits) * scene_valid * scene_recency).astype(jnp.bfloat16)

    return lax.map(one_scene, (pixels, valid_pix, recency))


def reproject(planes, rows_matrix, cols_matrix):
    half_done = jnp.einsum(
        "ncil,njl->ncij", planes, cols_matrix, preferred_element_type=jnp.float32
    ).astype(jnp.bfloat16)
    return jnp.einsum(
        "nij,ncjl->ncil", rows_matrix, half_done, preferred_element_type=jnp.float32
    ).astype(jnp.bfloat16)


def huber_merge(observed, weights):
    values = observed.astype(jnp.float32)
    plain = weights.astype(jnp.float32)[:, None, :]
    estimate = jnp.sum(plain * values, 0) / (jnp.sum(plain, 0) + prior_weight)
    for repeat in range(HUBER_ITERS):
        residual = values - estimate[None]
        huber_w = plain * huber_delta / jnp.maximum(jnp.abs(residual), huber_delta)
        estimate = jnp.sum(huber_w * values, 0) / (jnp.sum(huber_w, 0) + prior_weight)
    return estimate


def smooth_step(extended, first_col, total_cols):
    positions = first_col + jnp.arange(extended.shape[2] - 1)
    inside = ((positions >= 0) & (positions + 1 < total_cols)).astype(jnp.float32)
    across = extended[:, :, 1:] - extended[:, :, :-1]
    sideways = across / (1.0 + (across / edge_scale) ** 2) * inside
    centre = extended[:, :, 1:-1]
    upward_diff = centre[:, 1:, :] - centre[:, :-1, :]
    upward = upward_diff / (1.0 + (upward_diff / edge_scale) ** 2)
    zeros_row = jnp.zeros_like(upward[:, :1, :])
    vertical = jnp.concatenate([upward, zeros_row], 1) - jnp.concatenate([zeros_row, upward], 1)
    return centre + smooth_rate * (sideways[:, :, 1:] - sideways[:, :, :-1] + vertical)


def per_device(
    granules,
    valid_rows,
    scene_order,
    intersections,
    row_resample,
    col_resample,
    w_in,
    w_hidden,
    w_out,
):
    scenes, group_bands, pixel_count = granules.shape
    side_cells = valid_rows.shape[1]
    intersection_count = intersections.shape[1]
    tile_count = lax.axis_size("tile")
    band_count = lax.axis_size("band")
    recency = jnp.exp(1.4 * scene_order.astype(jnp.float32) / (scenes * tile_count) - 0.7)
    by_rows = lax.all_to_all(granules, "band", split_axis=2, concat_axis=1, tiled=True)
    row_count = side_cells // band_count
    valid_here = lax.dynamic_slice_in_dim(
        valid_rows, lax.axis_index("band") * row_count, row_count, 1
    )
    partial_weights = scene_weights(by_rows, valid_here, recency, w_in, w_hidden, w_out, side_cells)
    weights = lax.all_gather(partial_weights, "band", axis=1, tiled=True)
    plane_count = group_bands + 1
    planes = jnp.concatenate([granules, weights[:, None, :]], 1)
    entry_count = scenes * intersection_count
    capacity = (entry_count + tile_count - 1) // tile_count + 1
    buffer_rows = tile_count * capacity
    flat_dest = intersections.reshape(entry_count)
    onehot = (flat_dest[:, None] == jnp.arange(tile_count, dtype=jnp.int32)[None, :]).astype(
        jnp.int32
    )
    slot_rank = jnp.sum((jnp.cumsum(onehot, 0) - onehot) * onehot, 1)
    slot_index = flat_dest * capacity + slot_rank
    raw_planes = jnp.repeat(planes, intersection_count, axis=0)
    matrices = jnp.stack([row_resample, col_resample], 2).reshape(entry_count, 2, pixel_count)
    raw_out = (
        jnp.zeros((buffer_rows, plane_count, pixel_count), jnp.bfloat16)
        .at[slot_index]
        .set(raw_planes)
    )
    matrix_out = jnp.zeros((buffer_rows, 2, pixel_count), jnp.bfloat16).at[slot_index].set(matrices)
    raw_in, matrix_in = (
        lax.all_to_all(raw_out, "tile", split_axis=0, concat_axis=0, tiled=True),
        lax.all_to_all(matrix_out, "tile", split_axis=0, concat_axis=0, tiled=True),
    )
    matrix_in = matrix_in.reshape(buffer_rows, 2, side_cells, side_cells)
    incoming = reproject(
        raw_in.reshape(buffer_rows, plane_count, side_cells, side_cells),
        matrix_in[:, 0],
        matrix_in[:, 1],
    )
    incoming = incoming.reshape(buffer_rows, plane_count, pixel_count)
    estimate = huber_merge(incoming[:, :group_bands], incoming[:, group_bands])
    field = estimate.reshape(group_bands, side_cells, side_cells)
    first_col = lax.axis_index("tile") * side_cells
    total_cols = tile_count * side_cells
    for repeat in range(SMOOTH):
        extended = extended_2(field, (("tile", 2),), 1)
        field = smooth_step(extended, first_col - 1, total_cols)
    return field.reshape(group_bands, pixel_count)


def solution(mesh):
    return jax.shard_map(
        per_device,
        mesh=mesh,
        in_specs=(
            P("tile", "band", None),
            P("tile", None),
            P("tile"),
            P("tile", None),
            P("tile", None, None),
            P("tile", None, None),
            P(),
            P(),
            P(),
        ),
        out_specs=P("band", "tile"),
        check_vma=False,
    )
```

profile of v0, /device:TPU:1, one launch (start us, length us, event | category | flops | bytes accessed | tf_op | source)
XLA Modules:
  0.0 290.8 jit_solution(7013119373405686735)
XLA Ops:
  0.0 6.5 %copy.48 = bf16[16,4,4096]{0,1,2:T(4,128)(2,1)} copy(bf16[16,4,4096]{2,1,0:T(4,128)(2,1)} %param.11) | data formatting | bytes 1048576 | tf_op args[0]
  6.5 6.5 %reshape.137 = bf16[4,2,32768]{2,1,0:T(2,128)(2,1)} reshape(bf16[4096,4,16]{2,1,0:T(4,128)(2,1)} %bitcast.79) | data formatting | bytes 1048576
  13.0 4.3 %all-to-all-start = ((bf16[4,2,32768]{2,1,0:T(2,128)(2,1)}), bf16[4,2,32768]{2,1,0:T(2,128)(2,1)}, u32[]{:S(2)}, u32[]{:S(2)}) async-start(bf16[4,2,32768]{2,1,0:T(2,128)(2,1)} %reshape.137), calls=%async_computation | async-start | bytes 1048576 | tf_op jit(solution)/shard_map/all_to_all | solution.py:101
  18.3 0.8 stack.12
  19.1 0.8 stack.13
  19.9 2.4 pad_maximum_fusion.1
  22.3 2.2 broadcast_in_dim.40
  24.6 8.2 %scatter_fusion.1 = bf16[72,2,4096]{2,1,0:T(2,128)(2,1)} fusion(bf16[72,2,4096]{2,1,0:T(2,128)(2,1)} %broadcast_in_dim.40, s32[64]{0:T(128)S(1)} %fusion.56, bf16[64,2,4096]{2,1,0:T(2,128)(2,1)S(1)} %pad_maximum_fusion.1), kind=kCustom, calls=%fused_computation.1 | custom fusion | bytes 3145984 | tf_op jit(solution)/shard_map/scatter | solution.py:126
  32.8 6.3 %all-to-all-start.2 = ((bf16[72,2,4096]{2,1,0:T(2,128)(2,1)}), bf16[72,2,4096]{2,1,0:T(2,128)(2,1)S(1)}, u32[]{:S(2)}, u32[]{:S(2)}) async-start(bf16[72,2,4096]{2,1,0:T(2,128)(2,1)} %scatter_fusion.1), calls=%async_computation.2 | async-start | bytes 2359296 | tf_op jit(solution)/shard_map/all_to_all | solution.py:129
  39.1 5.4 %reshape.138 = bf16[4096,4,16]{2,1,0:T(4,128)(2,1)} reshape(bf16[4,2,32768]{2,1,0:T(2,128)(2,1)} %all-to-all-done) | data formatting | bytes 1048576
  44.5 6.1 %copy.49 = bf16[16,4,4,1024]{3,2,1,0:T(4,128)(2,1)S(1)} copy(bf16[16,4,4,1024]{0,2,3,1:T(4,128)(2,1)} %bitcast.78) | data formatting | bytes 1048576 | tf_op jit(solution)/shard_map/all_to_all | solution.py:101
  50.7 44.7 %while.10 = (s32[]{:T(128)}, bf16[16,1024]{1,0:T(8,128)(2,1)S(1)}, bf16[16,16,1024]{2,1,0:T(8,128)(2,1)S(1)}, bf16[16,256]{1,0:T(8,128)(2,1)S(1)}, bf16[2,256,25...) while((s32[]{:T(128)}, bf16[16,1024]{1,0:T(8,128)(2,1)S(1)}, ...), condition=%wide.region_3.4_spmd, body=%wide.region_2.3_spmd.sunk | while | flops 281285632 | bytes 1384577 | solution.py:48
  50.7 0.7 multiply_convert_fusion.9
  52.7 0.7 multiply_convert_fusion.10
  53.5 0.7 multiply_convert_fusion.9
  55.5 0.7 multiply_convert_fusion.10
  56.3 0.7 multiply_convert_fusion.9
  58.3 0.7 multiply_convert_fusion.10
  59.1 0.7 multiply_convert_fusion.9
  61.1 0.7 multiply_convert_fusion.10
  61.9 0.7 multiply_convert_fusion.9
  63.9 0.7 multiply_convert_fusion.10
  64.7 0.7 multiply_convert_fusion.9
  66.7 0.7 multiply_convert_fusion.10
  67.5 0.7 multiply_convert_fusion.9
  69.5 0.7 multiply_convert_fusion.10
  70.3 0.7 multiply_convert_fusion.9
  72.3 0.7 multiply_convert_fusion.10
  73.1 0.7 multiply_convert_fusion.9
  75.1 0.7 multiply_convert_fusion.10
  75.9 0.7 multiply_convert_fusion.9
  77.9 0.7 multiply_convert_fusion.10
  78.7 0.7 multiply_convert_fusion.9
  80.7 0.7 multiply_convert_fusion.10
  81.5 0.7 multiply_convert_fusion.9
  83.5 0.7 multiply_convert_fusion.10
  84.3 0.7 multiply_convert_fusion.9
  86.3 0.7 multiply_convert_fusion.10
  87.1 0.7 multiply_convert_fusion.9
  89.1 0.7 multiply_convert_fusion.10
  89.9 0.7 multiply_convert_fusion.9
  92.7 0.7 multiply_convert_fusion.9
  95.5 6.9 %all_gather.3 = bf16[16,4096]{1,0:T(8,128)(2,1)S(1)} all-gather(bf16[16,1024]{1,0:T(8,128)(2,1)S(1)} %get-tuple-element.47), channel_id=1, replica_groups=mesh['band'=4,'tile'=8] {'band'}, dimensions={1}, use_global_device_ids=true | all-gather | bytes 163840 | tf_op jit(solution)/shard_map/all_gather | solution.py:107
  103.1 2.5 broadcast_in_dim.20
  105.7 2.7 broadcast_in_dim.16
  108.4 12.0 %scatter_fusion = bf16[72,5,4096]{2,1,0:T(8,128)(2,1)} fusion(bf16[72,5,4096]{2,1,0:T(8,128)(2,1)} %broadcast_in_dim.16, s32[64]{0:T(128)S(1)} %fusion.56, bf16[64,5,4096]{2,1,0:T(8,128)(2,1)} %bitcast.77), kind=kCustom, calls=%fused_computation | custom fusion | bytes 7864576 | tf_op jit(solution)/shard_map/scatter | solution.py:124
  120.3 7.1 %all-to-all-start.1 = ((bf16[72,5,4096]{2,1,0:T(8,128)(2,1)}), bf16[72,5,4096]{2,1,0:T(8,128)(2,1)}, u32[]{:S(2)}, u32[]{:S(2)}) async-start(bf16[72,5,4096]{2,1,0:T(8,128)(2,1)} %scatter_fusion), calls=%async_computation.1 | async-start | bytes 9437184 | tf_op jit(solution)/shard_map/all_to_all | solution.py:128
  128.2 2.6 reshape.113
  130.7 101.2 %all-to-all-done.1 = bf16[72,5,4096]{2,1,0:T(8,128)(2,1)} async-done(((bf16[72,5,4096]{2,1,0:T(8,128)(2,1)}), bf16[72,5,4096]{2,1,0:T(8,128)(2,1)}, u32[]{:S(2)}, u32[]{:S(2)}) %all-to-all-start.1) | async-done | bytes 2949152 | tf_op jit(solution)/shard_map/all_to_all | solution.py:128
  232.0 10.6 %reshape.136 = bf16[72,5,64,64]{3,2,1,0:T(8,128)(2,1)} reshape(bf16[72,5,4096]{2,1,0:T(8,128)(2,1)} %all-to-all-done.1) | data formatting | bytes 5898240 | tf_op jit(solution)/shard_map/reshape | solution.py:133
  242.5 6.9 %convert_bitcast_fusion = bf16[72,5,64,64]{2,3,1,0:T(8,128)(2,1)} fusion(bf16[72,5,64,64]{3,2,1,0:T(8,128)(2,1)} %reshape.136, bf16[72,2,64,64]{3,2,0,1:T(8,128)(2,1)S(1)} %reshape.113), kind=kOutput, calls=%fused_computation.29 | convolution fusion | flops 380436480 | bytes 7077888 | tf_op jit(solution)/shard_map/nij,ncjl->ncil/dot_general | solution.py:55
  249.4 8.3 %copy.57 = bf16[72,5,64,64]{3,2,0,1:T(8,128)(2,1)} copy(bf16[72,5,64,64]{2,3,1,0:T(8,128)(2,1)} %convert_bitcast_fusion) | data formatting | bytes 5898240 | tf_op jit(solution)/shard_map/convert_element_type | solution.py:57
  257.7 7.6 %reshape.114 = bf16[72,5,4096]{2,0,1:T(8,128)(2,1)S(1)} reshape(bf16[72,5,64,64]{3,2,0,1:T(8,128)(2,1)} %copy.57) | data formatting | bytes 5898240 | tf_op jit(solution)/shard_map/reshape | solution.py:137
  266.2 1.8 fusion.45
  268.1 1.8 fusion.44
  269.9 1.8 fusion.43
  271.7 1.8 fusion.42
  273.8 2.8 collective-permute-start
  276.6 2.8 collective-permute-start.1
  280.1 1.2 collective-permute-done.1
  281.6 1.9 collective-permute-start.2
  283.6 4.4 %collective-permute-start.3 = (f32[4,64,1]{2,1,0:T(8,128)S(1)}, f32[4,64,1]{2,1,0:T(8,128)S(1)}, u32[]{:S(2)}, u32[]{:S(2)}) collective-permute-start(f32[4,64,1]{2,1,0:T(8,128)S(1)} %get-tuple-element.75), channel_id=1, source_target_pairs={{0,1},{1,2},{2,3},{3,4},{4,5},{5,6},{6,7},{8,9},{9,10},{10,11},{11... | collective-permute-start | bytes 3080 | tf_op jit(solution)/shard_map/ppermute | solution.py:21
  288.6 1.2 collective-permute-done.3
  290.1 0.7 reshape.115
  (157 shorter events, 28.1 us)
Async XLA Ops:
  0.0 17.3 %copy-start.3 = (s32[16,4]{0,1:T(4,128)S(1)}, s32[16,4]{0,1:T(4,128)}, u32[]{:S(2)}) copy-start(s32[16,4]{0,1:T(4,128)} %param.14) | copy-start | bytes 772
  0.0 17.4 %copy-start.4 = (s32[16,64]{1,0:T(8,128)S(1)}, s32[16,64]{1,0:T(8,128)}, u32[]{:S(2)}) copy-start(s32[16,64]{1,0:T(8,128)} %param.12) | copy-start | bytes 12292
  0.0 18.3 %copy-start.1 = (bf16[16,4,4096]{2,1,0:T(4,128)(2,1)S(1)}, bf16[16,4,4096]{2,1,0:T(4,128)(2,1)}, u32[]{:S(2)}) copy-start(bf16[16,4,4096]{2,1,0:T(4,128)(2,1)} %param.15) | copy-start | bytes 1572868
  6.5 12.6 %copy-start.2 = (bf16[16,4,4096]{2,1,0:T(4,128)(2,1)S(1)}, bf16[16,4,4096]{2,1,0:T(4,128)(2,1)}, u32[]{:S(2)}) copy-start(bf16[16,4,4096]{2,1,0:T(4,128)(2,1)} %param.16) | copy-start | bytes 1572868
  13.0 19.8 %all-to-all-start = ((bf16[4,2,32768]{2,1,0:T(2,128)(2,1)}), bf16[4,2,32768]{2,1,0:T(2,128)(2,1)}, u32[]{:S(2)}, u32[]{:S(2)}) async-start(bf16[4,2,32768]{2,1,0:T(2,128)(2,1)} %reshape.137), calls=%async_computation | async-start | bytes 1048576 | tf_op jit(solution)/shard_map/all_to_all | solution.py:101
  19.1 13.7 %copy-start.7 = (s32[16]{0:T(128)S(1)}, s32[16]{0:T(128)}, u32[]{:S(2)}) copy-start(s32[16]{0:T(128)} %param.13) | copy-start | bytes 196
  32.8 87.5 %all-to-all-start.2 = ((bf16[72,2,4096]{2,1,0:T(2,128)(2,1)}), bf16[72,2,4096]{2,1,0:T(2,128)(2,1)S(1)}, u32[]{:S(2)}, u32[]{:S(2)}) async-start(bf16[72,2,4096]{2,1,0:T(2,128)(2,1)} %scatter_fusion.1), calls=%async_computation.2 | async-start | bytes 2359296 | tf_op jit(solution)/shard_map/all_to_all | solution.py:129
  39.1 11.6 %copy-start.5 = (bf16[2,256,256]{2,1,0:T(8,128)(2,1)S(1)}, bf16[2,256,256]{2,1,0:T(8,128)(2,1)}, u32[]{:S(2)}) copy-start(bf16[2,256,256]{2,1,0:T(8,128)(2,1)} %param.18) | copy-start | bytes 786436
  39.1 11.6 %copy-start.6 = (bf16[16,256]{1,0:T(8,128)(2,1)S(1)}, bf16[16,256]{1,0:T(8,128)(2,1)}, u32[]{:S(2)}) copy-start(bf16[16,256]{1,0:T(8,128)(2,1)} %param.17) | copy-start | bytes 24580
  39.1 11.6 %copy-start.8 = (bf16[256]{0:T(256)(128)(2,1)S(1)}, bf16[256]{0:T(256)(128)(2,1)}, u32[]{:S(2)}) copy-start(bf16[256]{0:T(256)(128)(2,1)} %param.19) | copy-start | bytes 1540
  50.7 51.9 %copy-start = (bf16[16,4,4096]{2,1,0:T(4,128)(2,1)S(1)}, bf16[16,4,4096]{2,1,0:T(4,128)(2,1)}, u32[]{:S(2)}) copy-start(bf16[16,4,4096]{2,1,0:T(4,128)(2,1)} %param.11) | copy-start | bytes 1572868
  120.3 111.6 %all-to-all-start.1 = ((bf16[72,5,4096]{2,1,0:T(8,128)(2,1)}), bf16[72,5,4096]{2,1,0:T(8,128)(2,1)}, u32[]{:S(2)}, u32[]{:S(2)}) async-start(bf16[72,5,4096]{2,1,0:T(8,128)(2,1)} %scatter_fusion), calls=%async_computation.1 | async-start | bytes 9437184 | tf_op jit(solution)/shard_map/all_to_all | solution.py:128
  273.8 6.3 %collective-permute-start = (f32[4,64,1]{2,1,0:T(8,128)S(1)}, f32[4,64,1]{2,1,0:T(8,128)S(1)}, u32[]{:S(2)}, u32[]{:S(2)}) collective-permute-start(f32[4,64,1]{2,1,0:T(8,128)S(1)} %get-tuple-element.76), channel_id=1, source_target_pairs={{1,0},{2,1},{3,2},{4,3},{5,4},{6,5},{7,6},{9,8},{10,9},{11,10},{12... | collective-permute-start | bytes 3080 | tf_op jit(solution)/shard_map/ppermute | solution.py:24
  276.6 4.7 %collective-permute-start.1 = (f32[4,64,1]{2,1,0:T(8,128)S(1)}, f32[4,64,1]{2,1,0:T(8,128)S(1)}, u32[]{:S(2)}, u32[]{:S(2)}) collective-permute-start(f32[4,64,1]{2,1,0:T(8,128)S(1)} %get-tuple-element.77), channel_id=1, source_target_pairs={{0,1},{1,2},{2,3},{3,4},{4,5},{5,6},{6,7},{8,9},{9,10},{10,11},{11... | collective-permute-start | bytes 3080 | tf_op jit(solution)/shard_map/ppermute | solution.py:21
  281.6 7.0 %collective-permute-start.2 = (f32[4,64,1]{2,1,0:T(8,128)S(1)}, f32[4,64,1]{2,1,0:T(8,128)S(1)}, u32[]{:S(2)}, u32[]{:S(2)}) collective-permute-start(f32[4,64,1]{2,1,0:T(8,128)S(1)} %get-tuple-element.74), channel_id=1, source_target_pairs={{1,0},{2,1},{3,2},{4,3},{5,4},{6,5},{7,6},{9,8},{10,9},{11,10},{12... | collective-permute-start | bytes 3080 | tf_op jit(solution)/shard_map/ppermute | solution.py:24
  283.6 6.3 %collective-permute-start.3 = (f32[4,64,1]{2,1,0:T(8,128)S(1)}, f32[4,64,1]{2,1,0:T(8,128)S(1)}, u32[]{:S(2)}, u32[]{:S(2)}) collective-permute-start(f32[4,64,1]{2,1,0:T(8,128)S(1)} %get-tuple-element.75), channel_id=1, source_target_pairs={{0,1},{1,2},{2,3},{3,4},{4,5},{5,6},{6,7},{8,9},{9,10},{10,11},{11... | collective-permute-start | bytes 3080 | tf_op jit(solution)/shard_map/ppermute | solution.py:21
where the time goes:
time: 293 us; the launch traced here: 291 us
  waiting for transfers between devices  105 us (36%)
  local copies, waits for them, and re-layouts  97.5 us (33%)
  starting transfers between devices  29.5 us (10%)
  matrix products  27.5 us (9%)
  other arithmetic  23.3 us (8%)
  blocking collectives  6.89 us (2%)
    all_to_all x1, waiting for transfers between devices, per_device(): lax.all_to_all(raw_out, 'tile', split_axis=0, concat_axis=0, tiled=True)  101 us
    unnamed x22, local copies, waits for them, and re-layouts  18.5 us
    scatter x1, local copies, waits for them, and re-layouts, per_device(): raw_out = jnp.zeros((buffer_rows, plane_count, pixel_count), jnp.bfloat16...  12 us
    dot_general x16, matrix products, one_scene(): jnp.dot(hidden, w_hidden[repeat], preferred_element_type=jnp.float32)  11.9 us
    convert_element_type x16, other arithmetic, one_scene(): (jax.nn.sigmoid(-logits) * scene_valid * scene_recency).astype(jnp.bfloat16)  11.1 us
    dynamic_slice x32, local copies, waits for them, and re-layouts, scene_weights(): return lax.map(one_scene, (pixels, valid_pix, recency))  10.9 us
    reshape x1, local copies, waits for them, and re-layouts, per_device(): raw_in.reshape(buffer_rows, plane_count, side_cells, side_cells)  10.6 us
    dot_general x16, matrix products, one_scene(): logits = jnp.dot(hidden, w_out, preferred_element_type=jnp.float32)  8.79 us
  transfers between devices with their start and end apart: 7, of which 5 were waited for; matrix products, arithmetic and copies ran while one was open for 32% of the time, Pallas kernels for 0%

commit v1 on v0

v1 whole, which is shorter than its diff:
```python
import functools

import jax
import jax.numpy as jnp
import numpy as np
from jax import lax
from jax.experimental import pallas as pl
from jax.experimental.pallas import tpu as pltpu
from jax.sharding import PartitionSpec as P

HUBER_ITERS = 4
SMOOTH = 2
prior_weight = 0.25
huber_delta = 0.5
edge_scale = 1.0
smooth_rate = 0.2
BF = jnp.bfloat16
F32 = jnp.float32


def mlp_kernel(x_ref, scale_ref, w_in_ref, w_hid_ref, w_out_ref, out_ref):
    bands = [x_ref[b, 0] for b in range(x_ref.shape[0])]
    x = jnp.concatenate(bands, axis=0)

    def silu(t):
        return (t + t * jnp.tanh(t)).astype(BF)

    hidden = silu(jnp.dot(w_in_ref[...], x, preferred_element_type=F32))
    for layer in range(w_hid_ref.shape[0]):
        hidden = silu(jnp.dot(w_hid_ref[layer], hidden, preferred_element_type=F32))
    logits = jnp.dot(w_out_ref[...], hidden, preferred_element_type=F32)
    row = jax.nn.sigmoid(-logits[0:1])
    pieces = [row[:, i * 128 : (i + 1) * 128] for i in range(row.shape[1] // 128)]
    out_ref[0] = (jnp.concatenate(pieces, axis=0) * scale_ref[0]).astype(BF)


def cloud_weights(x, scale, w_in, w_hidden, w_out):
    groups, scenes, part, width = x.shape
    hid = w_in.shape[1]
    layers = w_hidden.shape[0]
    half = jnp.asarray(0.5, BF)
    w_in_t = (w_in * half).T
    w_hid_t = jnp.swapaxes(w_hidden * half, 1, 2)
    w_out_t = jnp.broadcast_to(w_out[None, :], (16, hid))
    lines = width // 128
    return pl.pallas_call(
        mlp_kernel,
        grid=(scenes,),
        in_specs=[
            pl.BlockSpec((groups, 1, part, width), lambda s: (0, s, 0, 0)),
            pl.BlockSpec((1, lines, 128), lambda s: (s, 0, 0)),
            pl.BlockSpec((hid, groups * part), lambda s: (0, 0)),
            pl.BlockSpec((layers, hid, hid), lambda s: (0, 0, 0)),
            pl.BlockSpec((16, hid), lambda s: (0, 0)),
        ],
        out_specs=pl.BlockSpec((1, lines, 128), lambda s: (s, 0, 0)),
        out_shape=jax.ShapeDtypeStruct((scenes, lines, 128), BF),
        compiler_params=pltpu.CompilerParams(vmem_limit_bytes=32 * 1024 * 1024),
        cost_estimate=pl.CostEstimate(
            flops=scenes * width * 2 * hid * (16 + layers * hid),
            bytes_accessed=4 * 1024 * 1024,
            transcendentals=scenes * width * hid * 3,
        ),
    )(x, scale, w_in_t, w_hid_t, w_out_t)


def merge_kernel(
    cap, scene_ref, present_ref, x_ref, w_ref, m_ref, q_ref, u_ref, v_ref, out_ref, y_ref, wt_ref
):
    source = pl.program_id(0)
    lane = lax.broadcasted_iota(jnp.int32, (32, 128), 1)
    low = lane < 64
    quarters = range(m_ref.shape[0])
    for r in range(cap):
        slot = source * cap + r
        scene = scene_ref[slot]
        planes = x_ref[scene]
        weight = jnp.concatenate([w_ref[0, b, scene] for b in quarters], axis=0)
        rows = jnp.concatenate([m_ref[b, r, 0:8] for b in quarters], axis=0)
        cols = jnp.concatenate([m_ref[b, r, 8:16] for b in quarters], axis=0).astype(F32)
        turned = pltpu.roll(cols, 64, 1)
        zero = jnp.zeros((32, 128), F32)
        first = jnp.concatenate([jnp.where(low, cols, zero), jnp.where(low, turned, zero)], 0)
        second = jnp.concatenate([jnp.where(low, zero, turned), jnp.where(low, zero, cols)], 0)
        first, second = first.astype(BF), second.astype(BF)
        blank = jnp.zeros((64, 128), BF)
        right = jnp.concatenate(
            [
                jnp.concatenate([first, blank], 1),
                jnp.concatenate([blank, first], 1),
                jnp.concatenate([second, blank], 1),
                jnp.concatenate([blank, second], 1),
            ],
            0,
        )
        left = jnp.concatenate(
            [
                jnp.concatenate([planes[0], planes[1]], 1),
                jnp.concatenate([planes[2], planes[3]], 1),
                jnp.concatenate([weight, weight], 1),
            ],
            0,
        )
        half = lax.dot_general(
            left, right, (((1,), (1,)), ((), ())), preferred_element_type=F32
        ).astype(BF)
        stacked = jnp.concatenate(
            [
                jnp.concatenate([half[p * 32 : p * 32 + 32, 0:128] for p in range(3)], 1),
                jnp.concatenate([half[p * 32 : p * 32 + 32, 128:256] for p in range(3)], 1),
            ],
            0,
        )
        spread = jnp.dot(rows, q_ref[...], preferred_element_type=F32).astype(BF)
        row_matrix = jnp.concatenate([spread[:, 0:64], spread[:, 128:192]], 0)
        moved = jnp.dot(row_matrix, stacked, preferred_element_type=F32)
        present = present_ref[slot].astype(F32)
        y_ref[slot] = moved[:, 0:256].astype(BF)
        wt_ref[slot] = (moved[:, 256:384] * present).astype(BF)

    @pl.when(source == pl.num_programs(0) - 1)
    def _():
        slots = y_ref.shape[0]
        chunk = 16

        def merge_rows(i, carry):
            here = pl.ds(pl.multiple_of(i * chunk, chunk), chunk)

            def load(n):
                y = y_ref[n, here, :].astype(F32)
                w = wt_ref[n, here, :].astype(F32)
                return y, jnp.concatenate([w, w], 1)

            def plain(n, sums):
                y, w = load(n)
                return sums[0] + w * y, sums[1] + w

            def robust(estimate, n, sums):
                y, w = load(n)
                size = jnp.maximum(jnp.abs(y - estimate), huber_delta)
                h = w * (huber_delta * pl.reciprocal(size, approx=True))
                return sums[0] + h * y, sums[1] + h

            empty = (jnp.zeros((chunk, 256), F32), jnp.zeros((chunk, 256), F32))
            top, bottom = lax.fori_loop(0, slots, plain, empty, unroll=4)
            estimate = top / (bottom + prior_weight)
            for _ in range(HUBER_ITERS):
                top, bottom = lax.fori_loop(
                    0, slots, functools.partial(robust, estimate), empty, unroll=4
                )
                estimate = top / (bottom + prior_weight)
            out_ref[here, :] = estimate
            return carry

        lax.fori_loop(0, 64 // chunk, merge_rows, 0)
        exact = lax.Precision.HIGHEST
        ordered = jnp.dot(u_ref[...], out_ref[...], precision=exact, preferred_element_type=F32)
        out_ref[:, 0:128] = jnp.dot(
            ordered[:, 0:128], v_ref[...], precision=exact, preferred_element_type=F32
        )
        out_ref[:, 128:256] = jnp.dot(
            ordered[:, 128:256], v_ref[...], precision=exact, preferred_element_type=F32
        )


def order_matrices():
    q = np.zeros((128, 256), np.float32)
    u = np.zeros((64, 64), np.float32)
    v = np.zeros((128, 128), np.float32)
    for n in range(64):
        place = (n % 2) * 32 + n // 2
        q[n, place] = 1
        q[64 + n, 128 + place] = 1
        u[n, place] = 1
        v[place, n] = 1
        v[64 + place, 64 + n] = 1
    return jnp.asarray(q, BF), jnp.asarray(u), jnp.asarray(v)


def merge(scene_of, present, planes, weights, matrices, cap):
    sources, quarters, scenes, lines, _ = weights.shape
    slots = sources * cap
    q, u, v = order_matrices()
    return pl.pallas_call(
        functools.partial(merge_kernel, cap),
        grid_spec=pltpu.PrefetchScalarGridSpec(
            num_scalar_prefetch=2,
            grid=(sources,),
            in_specs=[
                pl.BlockSpec((scenes, 4, 32, 128), lambda d, *_: (d, 0, 0, 0)),
                pl.BlockSpec((1, quarters, scenes, lines, 128), lambda d, *_: (d, 0, 0, 0, 0)),
                pl.BlockSpec((quarters, cap, 16, 128), lambda d, *_: (0, d, 0, 0)),
                pl.BlockSpec((128, 256), lambda d, *_: (0, 0)),
                pl.BlockSpec((64, 64), lambda d, *_: (0, 0)),
                pl.BlockSpec((128, 128), lambda d, *_: (0, 0)),
            ],
            out_specs=pl.BlockSpec((64, 256), lambda d, *_: (0, 0)),
            scratch_shapes=[
                pltpu.VMEM((slots, 64, 256), BF),
                pltpu.VMEM((slots, 64, 128), BF),
            ],
        ),
        out_shape=jax.ShapeDtypeStruct((64, 256), F32),
        compiler_params=pltpu.CompilerParams(vmem_limit_bytes=40 * 1024 * 1024),
        cost_estimate=pl.CostEstimate(
            flops=slots * 40_000_000, bytes_accessed=8 * 1024 * 1024, transcendentals=slots * 65536
        ),
    )(scene_of, present, planes, weights, matrices, q, u, v)


def smooth_step(extended, first_col, total_cols):
    positions = first_col + jnp.arange(extended.shape[2] - 1)
    inside = ((positions >= 0) & (positions + 1 < total_cols)).astype(F32)
    across = extended[:, :, 1:] - extended[:, :, :-1]
    sideways = across / (1.0 + (across / edge_scale) ** 2) * inside
    centre = extended[:, :, 1:-1]
    upward_diff = centre[:, 1:, :] - centre[:, :-1, :]
    upward = upward_diff / (1.0 + (upward_diff / edge_scale) ** 2)
    zeros_row = jnp.zeros_like(upward[:, :1, :])
    vertical = jnp.concatenate([upward, zeros_row], 1) - jnp.concatenate([zeros_row, upward], 1)
    return centre + smooth_rate * (sideways[:, :, 1:] - sideways[:, :, :-1] + vertical)


def per_device(
    granules,
    valid_rows,
    scene_order,
    intersections,
    row_resample,
    col_resample,
    w_in,
    w_hidden,
    w_out,
):
    scenes, group_bands, pixel_count = granules.shape
    side_cells = valid_rows.shape[1]
    top = intersections.shape[1]
    tile_count = lax.axis_size("tile")
    band_count = lax.axis_size("band")
    band = lax.axis_index("band")
    tile = lax.axis_index("tile")
    entry_count = scenes * top
    cap = (entry_count + tile_count - 1) // tile_count + 1
    part = pixel_count // band_count
    row_count = side_cells // band_count

    laid = granules.reshape(scenes, group_bands, pixel_count // 128, 128)
    planes = lax.all_gather(laid, "tile", axis=0, tiled=True)

    quarters = jnp.stack([granules[:, :, b * part : (b + 1) * part] for b in range(band_count)])
    by_rows = lax.all_to_all(quarters, "band", split_axis=0, concat_axis=0, tiled=True)
    recency = jnp.exp(1.4 * scene_order.astype(F32) / (scenes * tile_count) - 0.7)
    valid_here = lax.dynamic_slice_in_dim(valid_rows, band * row_count, row_count, 1).astype(F32)
    scale = valid_here * recency[:, None]
    scale = jnp.broadcast_to(scale[:, :, None], (scenes, row_count, side_cells))
    scale = scale.reshape(scenes, part // 128, 128)
    own_weights = cloud_weights(by_rows, scale, w_in, w_hidden, w_out)
    weights = lax.all_gather(own_weights, ("tile", "band"), axis=0, tiled=False)
    weights = weights.reshape((tile_count, band_count) + own_weights.shape)

    flat_dest = intersections.reshape(entry_count)
    is_dest = flat_dest[None, :] == jnp.arange(tile_count, dtype=jnp.int32)[:, None]
    rank = jnp.cumsum(is_dest.astype(jnp.int32), 1) - 1
    pick = is_dest[:, None, :] & (rank[:, None, :] == jnp.arange(cap)[None, :, None])
    pick = pick.reshape(tile_count * cap, entry_count).astype(BF)
    both = jnp.concatenate(
        [
            lax.dynamic_slice_in_dim(m, band * part, part, 2).reshape(entry_count, part)
            for m in (row_resample, col_resample)
        ],
        1,
    )
    sent = jnp.dot(pick, both, preferred_element_type=F32).astype(BF)
    sent = sent.reshape(tile_count * cap, 2 * part // 128, 128)
    got = lax.all_to_all(sent, "tile", split_axis=0, concat_axis=0, tiled=True)
    matrices = lax.all_gather(got, "band", axis=0, tiled=False)

    everywhere = lax.all_gather(intersections, "tile", axis=0, tiled=False)
    named = jnp.any(everywhere == tile, axis=2)
    order = jnp.cumsum(named.astype(jnp.int32), 1) - 1
    chosen = named[:, None, :] & (order[:, None, :] == jnp.arange(cap)[None, :, None])
    scene_of = jnp.sum(jnp.where(chosen, jnp.arange(scenes)[None, None, :], 0), 2)
    scene_of = scene_of.reshape(-1).astype(jnp.int32)
    present = jnp.any(chosen, 2).reshape(-1).astype(jnp.int32)

    estimate = merge(scene_of, present, planes, weights, matrices, cap)
    field = estimate.reshape(side_cells, group_bands, side_cells).transpose(1, 0, 2)

    forward = [(i, i + 1) for i in range(tile_count - 1)]
    backward = [(i + 1, i) for i in range(tile_count - 1)]
    low = lax.ppermute(field[:, :, side_cells - SMOOTH :], "tile", forward)
    high = lax.ppermute(field[:, :, :SMOOTH], "tile", backward)
    field = jnp.concatenate([low, field, high], 2)
    for step in range(SMOOTH):
        first_col = tile * side_cells - SMOOTH + step
        field = smooth_step(field, first_col, tile_count * side_cells)
    return field.reshape(group_bands, pixel_count)


def solution(mesh):
    return jax.shard_map(
        per_device,
        mesh=mesh,
        in_specs=(
            P("tile", "band", None),
            P("tile", None),
            P("tile"),
            P("tile", None),
            P("tile", None, None),
            P("tile", None, None),
            P(),
            P(),
            P(),
        ),
        out_specs=P("band", "tile"),
        check_vma=False,
    )
```

time: 293 us -> 208 us (0.71)
  local copies, waits for them, and re-layouts: 97.5 us -> 11.4 us
  Pallas kernels: 0 us -> 40.7 us
  matrix products: 27.5 us -> 0.28 us
  blocking collectives: 6.89 us -> 29.5 us
  starting transfers between devices: 29.5 us -> 9.15 us
  other arithmetic: 23.3 us -> 3.66 us
  between operations: 0.35 us -> 13.4 us
  waiting for transfers between devices: 105 us -> 99.6 us
    all_to_all x3 -> x1, waiting for transfers between devices: 101 us -> 10.6 us  [per_device(): lax.all_to_all(quarters, 'band', split_axis=0, concat_axis=0, tiled=True)]
    all_gather x0 -> x3, waiting for transfers between devices: none -> 87.1 us  [the longest x1 47.7 us: per_device(): planes = lax.all_gather(laid, 'tile', axis=0, tiled=True)]
    pallas_call x0 -> x2, Pallas kernels: none -> 40.7 us  [the longest x1 26.5 us: merge(): pl.pallas_call(functools.partial(merge_kernel, cap), grid_spec=pltpu.Pref...]
    dot_general x33 -> x1, matrix products: 27.5 us -> 0.28 us  [per_device(): sent = jnp.dot(pick, both, preferred_element_type=F32).astype(BF)]
    scatter x2 -> x0, local copies, waits for them, and re-layouts: 20.2 us -> none  [the longest x1 12 us: per_device(): raw_out = jnp.zeros((buffer_rows, plane_count, pixel_count), jnp.bfloat16...]
    reshape x4 -> x6, local copies, waits for them, and re-layouts: 20.9 us -> 1.69 us  [the longest x1 1.34 us: per_device(): laid = granules.reshape(scenes, group_bands, pixel_count // 128, 128)]
    all_to_all x0 -> x1, blocking collectives: none -> 16.2 us  [per_device(): got = lax.all_to_all(sent, 'tile', split_axis=0, concat_axis=0, tiled=True)]
    all_to_all x3 -> x1, starting transfers between devices: 17.7 us -> 3.47 us  [per_device(): lax.all_to_all(quarters, 'band', split_axis=0, concat_axis=0, tiled=True)]
  transfers between devices with their start and end apart: 7 -> 6, of which waited for: 5 -> 5; matrix products, arithmetic and copies ran while one was open for 32% -> 3% of each run, Pallas kernels for 0% -> 7%
where the time goes in v1:
time: 208 us
  waiting for transfers between devices  99.6 us (48%)
  Pallas kernels  40.7 us (20%)
  blocking collectives  29.5 us (14%)
  between operations  13.4 us (6%)
  local copies, waits for them, and re-layouts  11.4 us (5%)
  starting transfers between devices  9.15 us (4%)
  other arithmetic  3.66 us (2%)
    all_gather x1, waiting for transfers between devices, per_device(): planes = lax.all_gather(laid, 'tile', axis=0, tiled=True)  47.7 us
    all_gather x1, waiting for transfers between devices, per_device(): weights = lax.all_gather(own_weights, ('tile', 'band'), axis=0, tiled=False)  39.4 us
    pallas_call x1, Pallas kernels, merge(): pl.pallas_call(functools.partial(merge_kernel, cap), grid_spec=pltpu.Pref...  26.5 us
    all_to_all x1, blocking collectives, per_device(): got = lax.all_to_all(sent, 'tile', split_axis=0, concat_axis=0, tiled=True)  16.2 us
    pallas_call x1, Pallas kernels, cloud_weights(): pl.pallas_call(mlp_kernel, grid=(scenes,), in_specs=[pl.BlockSpec((groups...  14.2 us
    all_gather x1, blocking collectives, per_device(): everywhere = lax.all_gather(intersections, 'tile', axis=0, tiled=False)  13.3 us
    all_to_all x1, waiting for transfers between devices, per_device(): lax.all_to_all(quarters, 'band', split_axis=0, concat_axis=0, tiled=True)  10.6 us
    unnamed x29, local copies, waits for them, and re-layouts  5.66 us
  transfers between devices with their start and end apart: 6, of which 5 were waited for; matrix products, arithmetic and copies ran while one was open for 3% of the time, Pallas kernels for 7%

profile of v1, /device:TPU:1, one launch (start us, length us, event | category | flops | bytes accessed | tf_op | source)
XLA Modules:
  0.0 207.7 jit_solution(5984908950139948995)
XLA Ops:
  6.5 0.0 all-gather.12.cloned.1.call-start
  6.6 1.1 constant_dynamic-slice_fusion
  7.8 0.8 copy.39
  8.6 0.1 eq.67
  8.7 0.2 reduce_window_sum.23
  9.0 0.1 eq.74
  9.1 0.3 fusion
  9.4 16.2 %all_to_all.10 = bf16[72,16,128]{2,1,0:T(8,128)(2,1)} all-to-all(bf16[72,16,128]{2,1,0:T(8,128)(2,1)S(1)} %bitcast.23), channel_id=1, replica_groups=mesh['band'=4,'tile'=8] {'tile'}, dimensions={0} | all-to-all | bytes 589824 | tf_op jit(solution)/shard_map/all_to_all | solution.py:275
  25.6 0.0 all-gather.12.cloned.1.call-update
  25.6 1.3 slice_bitcast_fusion.3
  26.9 1.3 pad_maximum_fusion
  28.1 3.5 %all-to-all-start = ((bf16[4,16,4,1024]{3,2,1,0:T(4,128)(2,1)}), bf16[4,16,4,1024]{3,2,1,0:T(4,128)(2,1)S(1)}, u32[]{:S(2)}, u32[]{:S(2)}) async-start(bf16[4,16,4,1024]{3,2,1,0:T(4,128)(2,1)} %pad_maximum_fusion), calls=%async_computation | async-start | bytes 1048576 | tf_op jit(solution)/shard_map/all_to_all | solution.py:251
  31.6 0.0 all-gather.10.cloned.1.call-start
  31.7 0.0 copy-done.12
  31.7 0.0 copy-done.9
  31.7 0.1 convert_multiply_fusion
  31.8 0.1 broadcast_in_dim.14
  31.9 0.1 reshape.111.scale_ref
  32.0 0.0 copy-done.10
  32.0 0.1 copy.37
  32.1 0.0 copy-done.7
  32.1 0.1 copy.38
  32.3 10.6 %all-to-all-done.x_ref = bf16[4,16,4,1024]{3,2,1,0:T(4,128)(2,1)S(1)} async-done(((bf16[4,16,4,1024]{3,2,1,0:T(4,128)(2,1)}), bf16[4,16,4,1024]{3,2,1,0:T(4,128)(2,1)S(1)}, u32[]{:S(2)}, u32[]{:S(2)}) %all-to-all-start) | async-done | bytes 524320 | tf_op jit(solution)/shard_map/all_to_all | solution.py:251
  42.9 0.0 copy-done.11
  42.9 0.0 copy-start.8
  42.9 0.0 copy-start.3
  42.9 0.0 copy-start.4
  42.9 0.0 copy-start.5
  42.9 14.2 %shard_map.118 = bf16[16,8,128]{2,1,0:T(8,128)(2,1)} custom-call(bf16[4,16,4,1024]{3,2,1,0:T(4,128)(2,1)S(1)} %all-to-all-done.x_ref, f32[16,8,128]{2,1,0:T(8,128)S(1)} %reshape.111.scale_ref, bf16[256,16]{1,0:T(8,128)(2,1)S(1)} %bitcast.18, bf16[2,256,256]{2,1,0:T(8,128)(2,1)S(1)} %multiply_bitcast_fusion.w_hid_ref, ...), custom_call_target="tpu_custom_call" | custom-call | flops 4429185024 | bytes 4194304 | tf_op jit(solution)/shard_map/pallas_call | solution.py:46
  57.1 0.0 all-gather.10.cloned.1.call-update
  57.2 0.0 all-gather.8.cloned.1.call-start
  57.2 0.0 copy-done.6
  57.2 1.3 reshape.110
  58.6 0.0 all-gather.8.cloned.1.call-update
  58.6 13.3 %all-gather.3 = s32[8,16,4]{1,2,0:T(4,128)S(1)} all-gather(s32[1,16,4]{1,2,0:T(4,128)S(1)} %bitcast.24), channel_id=2, replica_groups=mesh['band'=4,'tile'=8] {'tile'}, dimensions={0}, use_global_device_ids=true | all-gather | bytes 2304 | tf_op jit(solution)/shard_map/all_gather | solution.py:278
  72.0 0.2 reduce_window_sum.22
  72.1 0.2 select_reduce_fusion
  72.4 0.1 copy.35
  72.5 0.1 reshape.109.scene_ref
  72.5 0.3 fusion.13
  72.8 0.1 copy.36
  72.9 0.1 reshape.118.present_ref
  73.0 0.0 all-gather.12.cloned.1.call-done
  73.0 39.4 %all-gather.10.cloned.1.call-done = bf16[512,8,128]{2,1,0:T(8,128)(2,1)} async-done(((bf16[16,8,128]{2,1,0:T(8,128)(2,1)}), bf16[512,8,128]{2,1,0:T(8,128)(2,1)}) %all-gather.10.cloned.1.call-update) | async-done | bytes 1048592 | tf_op jit(solution)/shard_map/all_gather | solution.py:258
  112.4 47.7 %all-gather.8.cloned.1.call-done.x_ref = bf16[128,4,32,128]{3,2,1,0:T(8,128)(2,1)} async-done(((bf16[16,4,32,128]{3,2,1,0:T(8,128)(2,1)}), bf16[128,4,32,128]{3,2,1,0:T(8,128)(2,1)}) %all-gather.8.cloned.1.call-update) | async-done | bytes 4194320 | tf_op jit(solution)/shard_map/all_gather | solution.py:248
  160.1 0.0 copy-done.4
  160.1 2.2 %copy-done = bf16[128,4,32,128]{3,2,1,0:T(8,128)(2,1)S(1)} copy-done((bf16[128,4,32,128]{3,2,1,0:T(8,128)(2,1)S(1)}, bf16[128,4,32,128]{3,2,1,0:T(8,128)(2,1)}, u32[]{:S(2)}) %copy-start) | copy-done | bytes 4194328
  162.3 1.3 copy-done.1
  163.6 1.2 copy-done.2
  164.8 26.5 %shard_map.119 = f32[64,256]{1,0:T(8,128)S(1)} custom-call(s32[72]{0:T(128)S(1)} %reshape.109.scene_ref, s32[72]{0:T(128)S(1)} %reshape.118.present_ref, bf16[128,4,32,128]{3,2,1,0:T(8,128)(2,1)S(1)} %copy-done, bf16[8,4,16,8,128]{4,3,2,1,0:T(8,128)(2,1)S(1)} %bitcast.20, bf16[4,72,16,128]{3,2,1,0:T(8,128)(2,1)S(1)} %bitcast.19, ...), custom_call_target="tpu_custom_call" | custom-call | flops 2880000000 | bytes 8388608 | tf_op jit(solution)/shard_map/pallas_call | solution.py:184
  191.3 0.1 reshape.116
  191.4 0.1 fusion.19
  191.5 2.2 %collective-permute-start.1 = (f32[4,64,2]{2,0,1:T(4,128)S(1)}, f32[4,64,2]{2,0,1:T(4,128)S(1)}, u32[]{:S(2)}, u32[]{:S(2)}) collective-permute-start(f32[4,64,2]{2,0,1:T(4,128)S(1)} %get-tuple-element.10), channel_id=1, source_target_pairs={{1,0},{2,1},{3,2},{4,3},{5,4},{6,5},{7,6},{9,8},{10,9},{11,10},{12... | collective-permute-start | bytes 6152 | tf_op jit(solution)/shard_map/ppermute | solution.py:292
  193.7 3.4 %collective-permute-start = (f32[4,64,2]{2,0,1:T(4,128)S(1)}, f32[4,64,2]{2,0,1:T(4,128)S(1)}, u32[]{:S(2)}, u32[]{:S(2)}) collective-permute-start(f32[4,64,2]{2,0,1:T(4,128)S(1)} %get-tuple-element.9), channel_id=1, source_target_pairs={{0,1},{1,2},{2,3},{3,4},{4,5},{5,6},{6,7},{8,9},{9,10},{10,11},{11... | collective-permute-start | bytes 6152 | tf_op jit(solution)/shard_map/ppermute | solution.py:291
  197.1 0.7 collective-permute-done.1
  197.8 1.2 collective-permute-done
  199.0 0.2 pad_maximum_fusion.1
  199.2 0.2 add_divide_fusion.3
  199.4 0.1 fusion.11
  199.6 0.2 fusion.9
  199.8 0.2 add_divide_fusion.2
  200.0 0.1 fusion.10
  200.2 0.2 fusion.6
  200.4 0.7 reshape.117
  (33 shorter events, 0.3 us)
Async XLA Ops:
  6.5 25.1 %copy-start.12 = (s32[16]{0:T(128)S(1)}, s32[16]{0:T(128)}, u32[]{:S(2)}) copy-start(s32[16]{0:T(128)} %param.14) | copy-start | bytes 196
  6.5 25.2 %copy-start.9 = (s32[16,64]{1,0:T(8,128)S(1)}, s32[16,64]{1,0:T(8,128)}, u32[]{:S(2)}) copy-start(s32[16,64]{1,0:T(8,128)} %param.13) | copy-start | bytes 12292
  6.5 25.4 %copy-start.10 = (bf16[16,256]{1,0:T(8,128)(2,1)S(1)}, bf16[16,256]{1,0:T(8,128)(2,1)}, u32[]{:S(2)}) copy-start(bf16[16,256]{1,0:T(8,128)(2,1)} %param.18) | copy-start | bytes 24580
  6.5 25.6 %copy-start.7 = (bf16[2,256,256]{2,1,0:T(8,128)(2,1)S(1)}, bf16[2,256,256]{2,1,0:T(8,128)(2,1)}, u32[]{:S(2)}) copy-start(bf16[2,256,256]{2,1,0:T(8,128)(2,1)} %param.19) | copy-start | bytes 786436
  6.5 36.3 %copy-start.11 = (bf16[256]{0:T(256)(128)(2,1)S(1)}, bf16[256]{0:T(256)(128)(2,1)}, u32[]{:S(2)}) copy-start(bf16[256]{0:T(256)(128)(2,1)} %param.20) | copy-start | bytes 1540
  6.5 66.5 %all-gather.12.cloned.1.call-start = ((), (), s32[]{:S(2)}) async-start(), calls=%async_computation.4 | async-start | bytes 1474560 | tf_op jit(solution)/shard_map/all_gather | solution.py:276
  28.1 14.7 %all-to-all-start = ((bf16[4,16,4,1024]{3,2,1,0:T(4,128)(2,1)}), bf16[4,16,4,1024]{3,2,1,0:T(4,128)(2,1)S(1)}, u32[]{:S(2)}, u32[]{:S(2)}) async-start(bf16[4,16,4,1024]{3,2,1,0:T(4,128)(2,1)} %pad_maximum_fusion), calls=%async_computation | async-start | bytes 1048576 | tf_op jit(solution)/shard_map/all_to_all | solution.py:251
  31.6 80.8 %all-gather.10.cloned.1.call-start = ((), (), s32[]{:S(2)}) async-start(), calls=%async_computation.3 | async-start | bytes 1081344 | tf_op jit(solution)/shard_map/all_gather | solution.py:258
  42.9 14.3 %copy-start.6 = (bf16[16,4,4096]{2,1,0:T(4,128)(2,1)S(1)}, bf16[16,4,4096]{2,1,0:T(4,128)(2,1)}, u32[]{:S(2)}) copy-start(bf16[16,4,4096]{2,1,0:T(4,128)(2,1)} %param.12) | copy-start | bytes 1572868
  42.9 15.7 %copy-start.8 = (s32[16,4]{0,1:T(4,128)S(1)}, s32[16,4]{0,1:T(4,128)}, u32[]{:S(2)}) copy-start(s32[16,4]{0,1:T(4,128)} %param.15) | copy-start | bytes 772
  42.9 117.2 %copy-start.3 = (bf16[128,256]{1,0:T(8,128)(2,1)S(1)}, bf16[128,256]{1,0:T(8,128)(2,1)}, u32[]{:S(2)}) copy-start(bf16[128,256]{1,0:T(8,128)(2,1)} %constant.19.clone.q_ref) | copy-start | bytes 196612
  42.9 117.2 %copy-start.4 = (f32[128,128]{1,0:T(8,128)S(1)}, f32[128,128]{1,0:T(8,128)}, u32[]{:S(2)}) copy-start(f32[128,128]{1,0:T(8,128)} %constant.74.clone.v_ref) | copy-start | bytes 196612
  42.9 117.2 %copy-start.5 = (f32[64,64]{1,0:T(8,128)S(1)}, f32[64,64]{1,0:T(8,128)}, u32[]{:S(2)}) copy-start(f32[64,64]{1,0:T(8,128)} %constant.20.clone.u_ref) | copy-start | bytes 49156
  57.2 102.9 %all-gather.8.cloned.1.call-start = ((), (), s32[]{:S(2)}) async-start(), calls=%async_computation.2 | async-start | bytes 4718592 | tf_op jit(solution)/shard_map/all_gather | solution.py:248
  160.1 2.2 %copy-start = (bf16[128,4,32,128]{3,2,1,0:T(8,128)(2,1)S(1)}, bf16[128,4,32,128]{3,2,1,0:T(8,128)(2,1)}, u32[]{:S(2)}) copy-start(bf16[128,4,32,128]{3,2,1,0:T(8,128)(2,1)} %all-gather.8.cloned.1.call-done.x_ref) | copy-start | bytes 12582916
  162.3 1.3 copy-start.1
  163.6 1.2 copy-start.2
  191.5 6.3 %collective-permute-start.1 = (f32[4,64,2]{2,0,1:T(4,128)S(1)}, f32[4,64,2]{2,0,1:T(4,128)S(1)}, u32[]{:S(2)}, u32[]{:S(2)}) collective-permute-start(f32[4,64,2]{2,0,1:T(4,128)S(1)} %get-tuple-element.10), channel_id=1, source_target_pairs={{1,0},{2,1},{3,2},{4,3},{5,4},{6,5},{7,6},{9,8},{10,9},{11,10},{12... | collective-permute-start | bytes 6152 | tf_op jit(solution)/shard_map/ppermute | solution.py:292
  193.7 5.3 %collective-permute-start = (f32[4,64,2]{2,0,1:T(4,128)S(1)}, f32[4,64,2]{2,0,1:T(4,128)S(1)}, u32[]{:S(2)}, u32[]{:S(2)}) collective-permute-start(f32[4,64,2]{2,0,1:T(4,128)S(1)} %get-tuple-element.9), channel_id=1, source_target_pairs={{0,1},{1,2},{2,3},{3,4},{4,5},{5,6},{6,7},{8,9},{9,10},{10,11},{11... | collective-permute-start | bytes 6152 | tf_op jit(solution)/shard_map/ppermute | solution.py:291
Sparse Core Ops, SparseCore 0:
  25.7 29.3 all-gather.11
  58.1 54.2 all-gather.9
  114.0 46.0 all-gather.7

commit v2 on v1

--- a/solution.py
+++ b/solution.py
@@ -18,24 +18,275 @@
 F32 = jnp.float32
 
 
-def mlp_kernel(x_ref, scale_ref, w_in_ref, w_hid_ref, w_out_ref, out_ref):
-    bands = [x_ref[b, 0] for b in range(x_ref.shape[0])]
-    x = jnp.concatenate(bands, axis=0)
-
-    def silu(t):
-        return (t + t * jnp.tanh(t)).astype(BF)
-
-    hidden = silu(jnp.dot(w_in_ref[...], x, preferred_element_type=F32))
-    for layer in range(w_hid_ref.shape[0]):
-        hidden = silu(jnp.dot(w_hid_ref[layer], hidden, preferred_element_type=F32))
-    logits = jnp.dot(w_out_ref[...], hidden, preferred_element_type=F32)
-    row = jax.nn.sigmoid(-logits[0:1])
-    pieces = [row[:, i * 128 : (i + 1) * 128] for i in range(row.shape[1] // 128)]
-    out_ref[0] = (jnp.concatenate(pieces, axis=0) * scale_ref[0]).astype(BF)
-
-
-def cloud_weights(x, scale, w_in, w_hidden, w_out):
-    groups, scenes, part, width = x.shape
+MESH = pl.DeviceIdType.MESH
+
+
+def exchange_kernel(
+    segment,
+    quarters_ref,
+    laid_ref,
+    sent_ref,
+    meta_ref,
+    scale_ref,
+    w_in_ref,
+    w_hid_ref,
+    w_out_ref,
+    planes_ref,
+    weights_ref,
+    matrices_ref,
+    codes_ref,
+    x_ref,
+    own_ref,
+    local_sems,
+    x_send,
+    x_recv,
+    right_send,
+    left_send,
+    plane_recv,
+    mat_send,
+    mat_recv,
+    code_send,
+    code_recv,
+    weight_send,
+    weight_recv,
+    mat_band_send,
+    mat_band_recv,
+    weight_band_send,
+    weight_band_recv,
+):
+    tiles = planes_ref.shape[0]
+    bands = quarters_ref.shape[0]
+    scenes = laid_ref.shape[0]
+    cap = sent_ref.shape[0] // tiles
+    tile = lax.axis_index("tile")
+    band = lax.axis_index("band")
+
+    def tile_peer(k):
+        return lax.rem(tile + k, tiles)
+
+    def tile_source(k):
+        return lax.rem(tile + tiles - k, tiles)
+
+    def band_peer(k):
+        return lax.rem(band + k, bands)
+
+    def for_tiles(first, body):
+        def step(k, carry):
+            body(k)
+            return carry
+
+        lax.fori_loop(first, tiles, step, 0)
+
+    barrier = pltpu.get_barrier_semaphore()
+    for_tiles(
+        1,
+        lambda k: pl.semaphore_signal(
+            barrier, inc=1, device_id={"tile": tile_peer(k)}, device_id_type=MESH
+        ),
+    )
+    for k in range(1, bands):
+        pl.semaphore_signal(barrier, inc=1, device_id={"band": band_peer(k)}, device_id_type=MESH)
+    pl.semaphore_wait(barrier, tiles - 1 + bands - 1)
+
+    def remote(src, dst, send, recv, where):
+        return pltpu.make_async_remote_copy(
+            src_ref=src,
+            dst_ref=dst,
+            send_sem=send,
+            recv_sem=recv,
+            device_id=where,
+            device_id_type=MESH,
+        )
+
+    def x_copy(peer, source):
+        return remote(
+            quarters_ref.at[peer], x_ref.at[source], x_send.at[peer], x_recv.at[source],
+            {"band": peer},
+        )
+
+    def plane_copy(shard, target, sems):
+        return remote(
+            planes_ref.at[shard], planes_ref.at[shard], sems.at[shard], plane_recv.at[shard],
+            {"tile": target},
+        )
+
+    def own_plane_copy(target, sems):
+        return remote(
+            laid_ref, planes_ref.at[tile], sems.at[tile], plane_recv.at[tile], {"tile": target}
+        )
+
+    def mat_copy(peer, source):
+        return remote(
+            sent_ref.at[pl.ds(peer * cap, cap)], matrices_ref.at[band, source],
+            mat_send.at[peer], mat_recv.at[source], {"tile": peer},
+        )
+
+    def code_copy(peer, source):
+        return remote(
+            meta_ref.at[peer], codes_ref.at[source], code_send.at[peer], code_recv.at[source],
+            {"tile": peer},
+        )
+
+    def weight_copy(peer, source):
+        return remote(
+            own_ref, weights_ref.at[band, source], weight_send.at[peer], weight_recv.at[source],
+            {"tile": peer},
+        )
+
+    def mat_band_copy(source, peer, owner):
+        return remote(
+            matrices_ref.at[owner, source], matrices_ref.at[owner, source],
+            mat_band_send.at[peer], mat_band_recv.at[owner], {"band": peer},
+        )
+
+    def weight_band_copy(source, peer, owner):
+        return remote(
+            weights_ref.at[owner, source], weights_ref.at[owner, source],
+            weight_band_send.at[peer], weight_band_recv.at[owner], {"band": peer},
+        )
+
+    for k in range(1, bands):
+        x_copy(band_peer(k), band).start()
+    x_local = pltpu.make_async_copy(quarters_ref.at[band], x_ref.at[band], local_sems.at[0])
+    x_local.start()
+
+    @pl.when(tile < tiles - 1)
+    def _():
+        own_plane_copy(tile + 1, right_send).start()
+
+    @pl.when(tile > 0)
+    def _():
+        own_plane_copy(tile - 1, left_send).start()
+
+    def first_sends(k):
+        mat_copy(tile_peer(k), tile).start()
+        code_copy(tile_peer(k), tile).start()
+
+    for_tiles(1, first_sends)
+    plane_local = pltpu.make_async_copy(laid_ref, planes_ref.at[tile], local_sems.at[1])
+    plane_local.start()
+    mat_local = pltpu.make_async_copy(
+        sent_ref.at[pl.ds(tile * cap, cap)], matrices_ref.at[band, tile], local_sems.at[2]
+    )
+    mat_local.start()
+    code_local = pltpu.make_async_copy(meta_ref.at[tile], codes_ref.at[tile], local_sems.at[3])
+    code_local.start()
+
+    def forward(s):
+        left, right = tile - s, tile + s
+
+        @pl.when(left >= 0)
+        def _():
+            plane_copy(left, tile, right_send).wait_recv()
+
+            @pl.when(tile < tiles - 1)
+            def _():
+                plane_copy(left, tile + 1, right_send).start()
+
+        @pl.when(right < tiles)
+        def _():
+            plane_copy(right, tile, left_send).wait_recv()
+
+            @pl.when(tile > 0)
+            def _():
+                plane_copy(right, tile - 1, left_send).start()
+
+    def network(scene, carry):
+        def silu(t):
+            return (t + t * jnp.tanh(t)).astype(BF)
+
+        x = jnp.concatenate([x_ref[b, scene] for b in range(bands)], axis=0)
+        hidden = silu(jnp.dot(w_in_ref[...], x, preferred_element_type=F32))
+        for layer in range(w_hid_ref.shape[0]):
+            hidden = silu(jnp.dot(w_hid_ref[layer], hidden, preferred_element_type=F32))
+        logits = jnp.dot(w_out_ref[...], hidden, preferred_element_type=F32)
+        row = jax.nn.sigmoid(-logits[0:1])
+        pieces = [row[:, i * 128 : (i + 1) * 128] for i in range(row.shape[1] // 128)]
+        own_ref[scene] = (jnp.concatenate(pieces, axis=0) * scale_ref[scene]).astype(BF)
+        return carry
+
+    def share_matrices():
+        mat_local.wait()
+        for k in range(1, bands):
+            mat_band_copy(tile, band_peer(k), band).start()
+
+        def share(k):
+            source = tile_source(k)
+            mat_copy(tile, source).wait_recv()
+            for j in range(1, bands):
+                mat_band_copy(source, band_peer(j), band).start()
+
+        for_tiles(1, share)
+
+    for k in range(1, bands):
+        source = lax.rem(band + bands - k, bands)
+        x_copy(source, source).wait_recv()
+    x_local.wait()
+    steps = 1
+    for start in range(0, scenes, segment):
+        lax.fori_loop(start, start + segment, network, 0)
+        if steps < tiles:
+            forward(steps)
+            steps += 1
+        if start == 2 * segment:
+            share_matrices()
+
+    weight_local = pltpu.make_async_copy(own_ref, weights_ref.at[band, tile], local_sems.at[4])
+    weight_local.start()
+    for_tiles(1, lambda k: weight_copy(tile_peer(k), tile).start())
+    weight_local.wait()
+    for k in range(1, bands):
+        weight_band_copy(tile, band_peer(k), band).start()
+
+    def share_weights(k):
+        source = tile_source(k)
+        weight_copy(tile, source).wait_recv()
+        for j in range(1, bands):
+            weight_band_copy(source, band_peer(j), band).start()
+
+    if steps < tiles:
+        forward(steps)
+        steps += 1
+    for_tiles(1, share_weights)
+    for_tiles(steps, forward)
+
+    plane_local.wait()
+    code_local.wait()
+
+    def finish(k):
+        code_copy(tile, tile_source(k)).wait_recv()
+        code_copy(tile_peer(k), tile).wait_send()
+        mat_copy(tile_peer(k), tile).wait_send()
+        weight_copy(tile_peer(k), tile).wait_send()
+
+    for_tiles(1, finish)
+
+    def finish_planes(shard):
+        @pl.when((shard <= tile) & (tile < tiles - 1))
+        def _():
+            plane_copy(shard, tile, right_send).wait_send()
+
+        @pl.when((shard >= tile) & (tile > 0))
+        def _():
+            plane_copy(shard, tile, left_send).wait_send()
+
+    for_tiles(0, finish_planes)
+    for k in range(1, bands):
+        peer = band_peer(k)
+        x_copy(peer, band).wait_send()
+        for ref, send, recv in (
+            (matrices_ref, mat_band_send, mat_band_recv),
+            (weights_ref, weight_band_send, weight_band_recv),
+        ):
+            whole = remote(ref.at[peer], ref.at[peer], send.at[peer], recv.at[peer], {"band": peer})
+            whole.wait_send()
+            whole.wait_recv()
+
+
+def exchange(quarters, laid, sent, meta, scale, w_in, w_hidden, w_out):
+    bands, scenes, part, width = quarters.shape
+    tiles = meta.shape[0]
+    cap = sent.shape[0] // tiles
     hid = w_in.shape[1]
     layers = w_hidden.shape[0]
     half = jnp.asarray(0.5, BF)
@@ -43,29 +294,36 @@
     w_hid_t = jnp.swapaxes(w_hidden * half, 1, 2)
     w_out_t = jnp.broadcast_to(w_out[None, :], (16, hid))
     lines = width // 128
+    anywhere = pl.BlockSpec(memory_space=pl.ANY)
+    vmem = pl.BlockSpec(memory_space=pltpu.VMEM)
+    dma = pltpu.SemaphoreType.DMA
     return pl.pallas_call(
-        mlp_kernel,
-        grid=(scenes,),
-        in_specs=[
-            pl.BlockSpec((groups, 1, part, width), lambda s: (0, s, 0, 0)),
-            pl.BlockSpec((1, lines, 128), lambda s: (s, 0, 0)),
-            pl.BlockSpec((hid, groups * part), lambda s: (0, 0)),
-            pl.BlockSpec((layers, hid, hid), lambda s: (0, 0, 0)),
-            pl.BlockSpec((16, hid), lambda s: (0, 0)),
+        functools.partial(exchange_kernel, max(1, scenes // 4)),
+        in_specs=[anywhere] * 4 + [vmem] * 4,
+        out_specs=[anywhere] * 4,
+        out_shape=[
+            jax.ShapeDtypeStruct((tiles,) + laid.shape, BF),
+            jax.ShapeDtypeStruct((bands, tiles, scenes, lines, 128), BF),
+            jax.ShapeDtypeStruct((bands, tiles, cap) + sent.shape[1:], BF),
+            jax.ShapeDtypeStruct(meta.shape, jnp.int32),
         ],
-        out_specs=pl.BlockSpec((1, lines, 128), lambda s: (s, 0, 0)),
-        out_shape=jax.ShapeDtypeStruct((scenes, lines, 128), BF),
-        compiler_params=pltpu.CompilerParams(vmem_limit_bytes=32 * 1024 * 1024),
-        cost_estimate=pl.CostEstimate(
-            flops=scenes * width * 2 * hid * (16 + layers * hid),
-            bytes_accessed=4 * 1024 * 1024,
-            transcendentals=scenes * width * hid * 3,
+        scratch_shapes=[
+            pltpu.VMEM(quarters.shape, BF),
+            pltpu.VMEM((scenes, lines, 128), BF),
+            dma((5,)),
+            dma((bands,)),
+            dma((bands,)),
+        ]
+        + [dma((tiles,))] * 9
+        + [dma((bands,))] * 4,
+        compiler_params=pltpu.CompilerParams(
+            collective_id=0, has_side_effects=True, vmem_limit_bytes=32 * 1024 * 1024
         ),
-    )(x, scale, w_in_t, w_hid_t, w_out_t)
+    )(quarters, laid, sent, meta, scale, w_in_t, w_hid_t, w_out_t)
 
 
 def merge_kernel(
-    cap, scene_ref, present_ref, x_ref, w_ref, m_ref, q_ref, u_ref, v_ref, out_ref, y_ref, wt_ref
+    cap, code_ref, x_ref, w_ref, m_ref, q_ref, u_ref, v_ref, out_ref, y_ref, wt_ref
 ):
     source = pl.program_id(0)
     lane = lax.broadcasted_iota(jnp.int32, (32, 128), 1)
@@ -73,11 +331,12 @@
     quarters = range(m_ref.shape[0])
     for r in range(cap):
         slot = source * cap + r
-        scene = scene_ref[slot]
-        planes = x_ref[scene]
-        weight = jnp.concatenate([w_ref[0, b, scene] for b in quarters], axis=0)
-        rows = jnp.concatenate([m_ref[b, r, 0:8] for b in quarters], axis=0)
-        cols = jnp.concatenate([m_ref[b, r, 8:16] for b in quarters], axis=0).astype(F32)
+        code = code_ref[slot]
+        scene = jnp.maximum(code, 0)
+        planes = x_ref[0, scene]
+        weight = jnp.concatenate([w_ref[b, 0, scene] for b in quarters], axis=0)
+        rows = jnp.concatenate([m_ref[b, 0, r, 0:8] for b in quarters], axis=0)
+        cols = jnp.concatenate([m_ref[b, 0, r, 8:16] for b in quarters], axis=0).astype(F32)
         turned = pltpu.roll(cols, 64, 1)
         zero = jnp.zeros((32, 128), F32)
         first = jnp.concatenate([jnp.where(low, cols, zero), jnp.where(low, turned, zero)], 0)
@@ -114,7 +373,7 @@
         spread = jnp.dot(rows, q_ref[...], preferred_element_type=F32).astype(BF)
         row_matrix = jnp.concatenate([spread[:, 0:64], spread[:, 128:192]], 0)
         moved = jnp.dot(row_matrix, stacked, preferred_element_type=F32)
-        present = present_ref[slot].astype(F32)
+        present = jnp.where(code >= 0, 1.0, 0.0)
         y_ref[slot] = moved[:, 0:256].astype(BF)
         wt_ref[slot] = (moved[:, 256:384] * present).astype(BF)
 
@@ -177,19 +436,20 @@
     return jnp.asarray(q, BF), jnp.asarray(u), jnp.asarray(v)
 
 
-def merge(scene_of, present, planes, weights, matrices, cap):
-    sources, quarters, scenes, lines, _ = weights.shape
+def merge(codes, planes, weights, matrices):
+    quarters, sources, scenes, lines, _ = weights.shape
+    cap = matrices.shape[2]
     slots = sources * cap
     q, u, v = order_matrices()
     return pl.pallas_call(
         functools.partial(merge_kernel, cap),
         grid_spec=pltpu.PrefetchScalarGridSpec(
-            num_scalar_prefetch=2,
+            num_scalar_prefetch=1,
             grid=(sources,),
             in_specs=[
-                pl.BlockSpec((scenes, 4, 32, 128), lambda d, *_: (d, 0, 0, 0)),
-                pl.BlockSpec((1, quarters, scenes, lines, 128), lambda d, *_: (d, 0, 0, 0, 0)),
-                pl.BlockSpec((quarters, cap, 16, 128), lambda d, *_: (0, d, 0, 0)),
+                pl.BlockSpec((1, scenes, 4, 32, 128), lambda d, *_: (d, 0, 0, 0, 0)),
+                pl.BlockSpec((quarters, 1, scenes, lines, 128), lambda d, *_: (0, d, 0, 0, 0)),
+                pl.BlockSpec((quarters, 1, cap, 16, 128), lambda d, *_: (0, d, 0, 0, 0)),
                 pl.BlockSpec((128, 256), lambda d, *_: (0, 0)),
                 pl.BlockSpec((64, 64), lambda d, *_: (0, 0)),
                 pl.BlockSpec((128, 128), lambda d, *_: (0, 0)),
@@ -205,7 +465,7 @@
         cost_estimate=pl.CostEstimate(
             flops=slots * 40_000_000, bytes_accessed=8 * 1024 * 1024, transcendentals=slots * 65536
         ),
-    )(scene_of, present, planes, weights, matrices, q, u, v)
+    )(codes, planes, weights, matrices, q, u, v)
 
 
 def smooth_step(extended, first_col, total_cols):
@@ -245,23 +505,19 @@
     row_count = side_cells // band_count
 
     laid = granules.reshape(scenes, group_bands, pixel_count // 128, 128)
-    planes = lax.all_gather(laid, "tile", axis=0, tiled=True)
-
     quarters = jnp.stack([granules[:, :, b * part : (b + 1) * part] for b in range(band_count)])
-    by_rows = lax.all_to_all(quarters, "band", split_axis=0, concat_axis=0, tiled=True)
     recency = jnp.exp(1.4 * scene_order.astype(F32) / (scenes * tile_count) - 0.7)
     valid_here = lax.dynamic_slice_in_dim(valid_rows, band * row_count, row_count, 1).astype(F32)
     scale = valid_here * recency[:, None]
     scale = jnp.broadcast_to(scale[:, :, None], (scenes, row_count, side_cells))
     scale = scale.reshape(scenes, part // 128, 128)
-    own_weights = cloud_weights(by_rows, scale, w_in, w_hidden, w_out)
-    weights = lax.all_gather(own_weights, ("tile", "band"), axis=0, tiled=False)
-    weights = weights.reshape((tile_count, band_count) + own_weights.shape)
-
     flat_dest = intersections.reshape(entry_count)
     is_dest = flat_dest[None, :] == jnp.arange(tile_count, dtype=jnp.int32)[:, None]
     rank = jnp.cumsum(is_dest.astype(jnp.int32), 1) - 1
     pick = is_dest[:, None, :] & (rank[:, None, :] == jnp.arange(cap)[None, :, None])
+    scene_ids = (jnp.arange(entry_count, dtype=jnp.int32) // top + 1)[None, None, :]
+    code = jnp.sum(jnp.where(pick, scene_ids, 0), 2) - 1
+    meta = jnp.zeros((tile_count, 8, 128), jnp.int32).at[:, 0, :cap].set(code)
     pick = pick.reshape(tile_count * cap, entry_count).astype(BF)
     both = jnp.concatenate(
         [
@@ -272,18 +528,10 @@
     )
     sent = jnp.dot(pick, both, preferred_element_type=F32).astype(BF)
     sent = sent.reshape(tile_count * cap, 2 * part // 128, 128)
-    got = lax.all_to_all(sent, "tile", split_axis=0, concat_axis=0, tiled=True)
-    matrices = lax.all_gather(got, "band", axis=0, tiled=False)
-
-    everywhere = lax.all_gather(intersections, "tile", axis=0, tiled=False)
-    named = jnp.any(everywhere == tile, axis=2)
-    order = jnp.cumsum(named.astype(jnp.int32), 1) - 1
-    chosen = named[:, None, :] & (order[:, None, :] == jnp.arange(cap)[None, :, None])
-    scene_of = jnp.sum(jnp.where(chosen, jnp.arange(scenes)[None, None, :], 0), 2)
-    scene_of = scene_of.reshape(-1).astype(jnp.int32)
-    present = jnp.any(chosen, 2).reshape(-1).astype(jnp.int32)
-
-    estimate = merge(scene_of, present, planes, weights, matrices, cap)
+    planes, weights, matrices, codes = exchange(
+        quarters, laid, sent, meta, scale, w_in, w_hidden, w_out
+    )
+    estimate = merge(codes[:, 0, :cap].reshape(-1), planes, weights, matrices)
     field = estimate.reshape(side_cells, group_bands, side_cells).transpose(1, 0, 2)
 
     forward = [(i, i + 1) for i in range(tile_count - 1)]

time: 208 us -> 109 us (0.52)
  waiting for transfers between devices: 99.6 us -> 4.32 us
  Pallas kernels: 40.7 us -> 83.1 us
  blocking collectives: 29.5 us -> 0 us
  between operations: 13.4 us -> 0.36 us
  starting transfers between devices: 9.15 us -> 5.37 us
    all_gather x3 -> x0, waiting for transfers between devices: 87.1 us -> none  [the longest x1 47.7 us: per_device(): planes = lax.all_gather(laid, 'tile', axis=0, tiled=True)]
    pallas_call x1, Pallas kernels: 14.2 us -> 56.6 us  [exchange(): pl.pallas_call(functools.partial(exchange_kernel, max(1, scenes // 4)), i...]
    all_to_all x1 -> x0, blocking collectives: 16.2 us -> none  [per_device(): got = lax.all_to_all(sent, 'tile', split_axis=0, concat_axis=0, tiled=True)]
    all_gather x1 -> x0, blocking collectives: 13.3 us -> none  [per_device(): everywhere = lax.all_gather(intersections, 'tile', axis=0, tiled=False)]
    all_to_all x1 -> x0, waiting for transfers between devices: 10.6 us -> none  [per_device(): lax.all_to_all(quarters, 'band', split_axis=0, concat_axis=0, tiled=True)]
    ppermute x1, waiting for transfers between devices: 0.69 us -> 4.31 us  [per_device(): high = lax.ppermute(field[:, :, :SMOOTH], 'tile', backward)]
    all_to_all x1 -> x0, starting transfers between devices: 3.47 us -> none  [per_device(): lax.all_to_all(quarters, 'band', split_axis=0, concat_axis=0, tiled=True)]
    unnamed x29 -> x23, local copies, waits for them, and re-layouts: 5.66 us -> 6.68 us
  transfers between devices with their start and end apart: 6 -> 2, of which waited for: 5 -> 1; matrix products, arithmetic and copies ran while one was open for 3% -> 0% of each run, Pallas kernels for 7% -> 0%
where the time goes in v2:
time: 109 us; the launch traced here: 108 us
  Pallas kernels  83.1 us (76%)
  local copies, waits for them, and re-layouts  12.4 us (11%)
  starting transfers between devices  5.37 us (5%)
  waiting for transfers between devices  4.32 us (4%)
  other arithmetic  2.36 us (2%)
    pallas_call x1, Pallas kernels, exchange(): pl.pallas_call(functools.partial(exchange_kernel, max(1, scenes // 4)), i...  56.6 us
    pallas_call x1, Pallas kernels, merge(): pl.pallas_call(functools.partial(merge_kernel, cap), grid_spec=pltpu.Pref...  26.5 us
    unnamed x23, local copies, waits for them, and re-layouts  6.68 us
    ppermute x1, waiting for transfers between devices, per_device(): high = lax.ppermute(field[:, :, :SMOOTH], 'tile', backward)  4.31 us
    ppermute x1, starting transfers between devices, per_device(): low = lax.ppermute(field[:, :, side_cells - SMOOTH:], 'tile', forward)  3.45 us
  transfers between devices with their start and end apart: 2, of which 1 were waited for; matrix products, arithmetic and copies ran while one was open for 0% of the time, Pallas kernels for 0%

profile of v2, /device:TPU:1, one launch (start us, length us, event | category | flops | bytes accessed | tf_op | source)
XLA Modules:
  0.0 108.2 jit_solution(17760114577719920420)
XLA Ops:
  0.0 0.0 copy-start.9
  0.0 0.0 copy-start.6
  0.0 0.0 copy-start.5
  0.0 0.0 copy-start.7
  0.0 0.0 copy-start.8
  0.0 1.4 %slice_bitcast_fusion.3 = (bf16[1,16,4,1024]{3,2,1,0:T(4,128)(2,1)S(1)}, bf16[1,16,4,1024]{3,2,1,0:T(4,128)(2,1)S(1)}, bf16[1,16,4,1024]{3,2,1,0:T(4,128)(2,1)S(1)}, bf16[1,16,4,1024]{3,2,1,0:T(4,128)(2,1)S(1)}) fusion(bf16[16,4,4096]{2,1,0:T(4,128)(2,1)} %param.14), kind=kLoop, calls=%fused_computation.25 | loop fusion | bytes 1048576 | tf_op jit(solution)/shard_map/stack | solution.py:508
  1.4 0.0 copy-start.2
  1.4 1.6 %reshape.147.laid_ref = bf16[16,4,32,128]{3,2,1,0:T(8,128)(2,1)S(1)} reshape(bf16[16,4,4096]{2,1,0:T(4,128)(2,1)} %param.14) | data formatting | bytes 1048576 | tf_op jit(solution)/shard_map/reshape | solution.py:507
  3.1 1.1 constant_dynamic-slice_fusion
  4.2 0.8 copy.25
  5.0 0.1 eq.47
  5.1 0.2 reduce_window_sum.11
  5.4 0.1 eq.54
  5.5 0.3 fusion
  5.8 0.0 copy-done.9
  5.8 0.0 copy-done.6
  5.8 0.1 convert_multiply_fusion
  5.9 0.1 broadcast_in_dim.14
  6.0 0.1 reshape.151.scale_ref
  6.1 0.2 select_reduce_fusion
  6.3 0.0 copy-done.5
  6.4 0.1 copy.28
  6.5 0.0 copy-done.7
  6.5 0.1 copy.27
  6.7 0.5 pad_maximum_fusion.quarters_ref
  7.1 0.0 copy-done.8
  7.2 56.6 %shard_map.118 = (bf16[8,16,4,32,128]{4,3,2,1,0:T(8,128)(2,1)S(1)}, bf16[4,8,16,8,128]{4,3,2,1,0:T(8,128)(2,1)S(1)}, bf16[4,8,9,16,128]{4,3,2,1,0:T(8,128)(2,1)S(1)}, s32[8,8,128]{2,1,0:T(8,128)S(1)}) custom-call(bf16[4,16,4,1024]{3,2,1,0:T(4,128)(2,1)S(1)} %pad_maximum_fusion.quarters_ref, bf16[16,4,32,128]{3,2,1,0:T(8,128)(2,1)S(1)} %reshape.147.laid_ref, ...), custom_call_target="tpu_custom_call" | custom-call | tf_op jit(solution)/shard_map/pallas_call | solution.py:300
  63.8 0.0 copy-start
  63.8 1.9 %copy-done = bf16[8,16,4,32,128]{4,3,2,1,0:T(8,128)(2,1)} copy-done((bf16[8,16,4,32,128]{4,3,2,1,0:T(8,128)(2,1)}, bf16[8,16,4,32,128]{4,3,2,1,0:T(8,128)(2,1)S(1)}, u32[]{:S(2)}) %copy-start) | copy-done | bytes 4194328
  65.7 0.1 reshape_squeeze.3.code_ref
  65.8 0.0 copy-done.2
  65.8 0.0 copy-start.1
  65.8 2.2 %copy-done.1 = bf16[8,16,4,32,128]{4,3,2,1,0:T(8,128)(2,1)S(1)} copy-done((bf16[8,16,4,32,128]{4,3,2,1,0:T(8,128)(2,1)S(1)}, bf16[8,16,4,32,128]{4,3,2,1,0:T(8,128)(2,1)}, u32[]{:S(2)}) %copy-start.1) | copy-done | bytes 4194328
  68.0 0.0 copy-start.3
  68.0 0.8 copy-done.3
  68.8 0.0 copy-start.4
  68.8 0.8 copy-done.4
  69.6 26.5 %shard_map.119 = f32[64,256]{1,0:T(8,128)S(1)} custom-call(s32[72]{0:T(128)S(1)} %reshape_squeeze.3.code_ref, bf16[8,16,4,32,128]{4,3,2,1,0:T(8,128)(2,1)S(1)} %copy-done.1, bf16[4,8,16,8,128]{4,3,2,1,0:T(8,128)(2,1)S(1)} %get-tuple-element.23.w_ref, bf16[4,8,9,16,128]{4,3,2,1,0:T(8,128)(2,1)S(1)} %get-tuple-element.24.m_ref, ...), custom_call_target="tpu_custom_call" | custom-call | flops 2880000000 | bytes 8388608 | tf_op jit(solution)/shard_map/pallas_call | solution.py:444
  96.1 0.1 reshape.152
  96.2 0.1 fusion.19
  96.4 3.5 %collective-permute-start = (f32[4,64,2]{2,0,1:T(4,128)S(1)}, f32[4,64,2]{2,0,1:T(4,128)S(1)}, u32[]{:S(2)}, u32[]{:S(2)}) collective-permute-start(f32[4,64,2]{2,0,1:T(4,128)S(1)} %get-tuple-element.29), channel_id=1, source_target_pairs={{0,1},{1,2},{2,3},{3,4},{4,5},{5,6},{6,7},{8,9},{9,10},{10,11},{11... | collective-permute-start | bytes 6152 | tf_op jit(solution)/shard_map/ppermute | solution.py:539
  99.8 1.9 %collective-permute-start.1 = (f32[4,64,2]{2,0,1:T(4,128)S(1)}, f32[4,64,2]{2,0,1:T(4,128)S(1)}, u32[]{:S(2)}, u32[]{:S(2)}) collective-permute-start(f32[4,64,2]{2,0,1:T(4,128)S(1)} %get-tuple-element.30), channel_id=1, source_target_pairs={{1,0},{2,1},{3,2},{4,3},{5,4},{6,5},{7,6},{9,8},{10,9},{11,10},{12... | collective-permute-start | bytes 6152 | tf_op jit(solution)/shard_map/ppermute | solution.py:540
  101.8 0.0 collective-permute-done
  101.8 4.3 %collective-permute-done.1 = f32[4,64,2]{2,0,1:T(4,128)S(1)} collective-permute-done((f32[4,64,2]{2,0,1:T(4,128)S(1)}, f32[4,64,2]{2,0,1:T(4,128)S(1)}, u32[]{:S(2)}, u32[]{:S(2)}) %collective-permute-start.1) | collective-permute-done | bytes 2080 | tf_op jit(solution)/shard_map/ppermute | solution.py:540
  106.1 0.2 pad_maximum_fusion.1
  106.3 0.2 add_divide_fusion.3
  106.6 0.1 fusion.11
  106.7 0.2 fusion.9
  106.9 0.2 add_divide_fusion.2
  107.1 0.1 fusion.10
  107.3 0.2 fusion.6
  107.5 0.7 reshape.153
  (21 shorter events, 0.3 us)
Async XLA Ops:
  0.0 5.8 %copy-start.9 = (s32[16]{0:T(128)S(1)}, s32[16]{0:T(128)}, u32[]{:S(2)}) copy-start(s32[16]{0:T(128)} %param.16) | copy-start | bytes 196
  0.0 5.8 %copy-start.6 = (s32[16,64]{1,0:T(8,128)S(1)}, s32[16,64]{1,0:T(8,128)}, u32[]{:S(2)}) copy-start(s32[16,64]{1,0:T(8,128)} %param.15) | copy-start | bytes 12292
  0.0 6.3 %copy-start.5 = (bf16[2,256,256]{2,1,0:T(8,128)(2,1)S(1)}, bf16[2,256,256]{2,1,0:T(8,128)(2,1)}, u32[]{:S(2)}) copy-start(bf16[2,256,256]{2,1,0:T(8,128)(2,1)} %param.21) | copy-start | bytes 786436
  0.0 6.5 %copy-start.7 = (bf16[16,256]{1,0:T(8,128)(2,1)S(1)}, bf16[16,256]{1,0:T(8,128)(2,1)}, u32[]{:S(2)}) copy-start(bf16[16,256]{1,0:T(8,128)(2,1)} %param.20) | copy-start | bytes 24580
  0.0 7.1 %copy-start.8 = (bf16[256]{0:T(256)(128)(2,1)S(1)}, bf16[256]{0:T(256)(128)(2,1)}, u32[]{:S(2)}) copy-start(bf16[256]{0:T(256)(128)(2,1)} %param.22) | copy-start | bytes 1540
  1.4 64.4 %copy-start.2 = (bf16[128,256]{1,0:T(8,128)(2,1)S(1)}, bf16[128,256]{1,0:T(8,128)(2,1)}, u32[]{:S(2)}) copy-start(bf16[128,256]{1,0:T(8,128)(2,1)} %constant.112.clone.q_ref) | copy-start | bytes 196612
  63.8 1.9 %copy-start = (bf16[8,16,4,32,128]{4,3,2,1,0:T(8,128)(2,1)}, bf16[8,16,4,32,128]{4,3,2,1,0:T(8,128)(2,1)S(1)}, u32[]{:S(2)}) copy-start(bf16[8,16,4,32,128]{4,3,2,1,0:T(8,128)(2,1)S(1)} %get-tuple-element.22.x_ref) | copy-start | bytes 12582916
  65.8 2.2 %copy-start.1 = (bf16[8,16,4,32,128]{4,3,2,1,0:T(8,128)(2,1)S(1)}, bf16[8,16,4,32,128]{4,3,2,1,0:T(8,128)(2,1)}, u32[]{:S(2)}) copy-start(bf16[8,16,4,32,128]{4,3,2,1,0:T(8,128)(2,1)} %copy-done) | copy-start | bytes 12582916
  68.0 0.8 copy-start.3
  68.8 0.8 copy-start.4
  96.4 5.4 %collective-permute-start = (f32[4,64,2]{2,0,1:T(4,128)S(1)}, f32[4,64,2]{2,0,1:T(4,128)S(1)}, u32[]{:S(2)}, u32[]{:S(2)}) collective-permute-start(f32[4,64,2]{2,0,1:T(4,128)S(1)} %get-tuple-element.29), channel_id=1, source_target_pairs={{0,1},{1,2},{2,3},{3,4},{4,5},{5,6},{6,7},{8,9},{9,10},{10,11},{11... | collective-permute-start | bytes 6152 | tf_op jit(solution)/shard_map/ppermute | solution.py:539
  99.8 6.3 %collective-permute-start.1 = (f32[4,64,2]{2,0,1:T(4,128)S(1)}, f32[4,64,2]{2,0,1:T(4,128)S(1)}, u32[]{:S(2)}, u32[]{:S(2)}) collective-permute-start(f32[4,64,2]{2,0,1:T(4,128)S(1)} %get-tuple-element.30), channel_id=1, source_target_pairs={{1,0},{2,1},{3,2},{4,3},{5,4},{6,5},{7,6},{9,8},{10,9},{11,10},{12... | collective-permute-start | bytes 6152 | tf_op jit(solution)/shard_map/ppermute | solution.py:540

commit v3 on v2

--- a/solution.py
+++ b/solution.py
@@ -12,10 +12,116 @@
 SMOOTH = 2
 prior_weight = 0.25
 huber_delta = 0.5
-edge_scale = 1.0
 smooth_rate = 0.2
 BF = jnp.bfloat16
 F32 = jnp.float32
+
+
+def reproject_slot(r, slot, code_ref, x_ref, w_ref, m_ref, q_ref, y_ref, wt_ref):
+    lane = lax.broadcasted_iota(jnp.int32, (32, 128), 1)
+    low = lane < 64
+    quarters = range(m_ref.shape[0])
+    code = code_ref[0, r]
+    scene = jnp.maximum(code, 0)
+    present = jnp.minimum(code + 1, 1).astype(F32)
+    planes = x_ref[scene]
+    weight = jnp.concatenate([w_ref[b, scene] for b in quarters], axis=0)
+    rows = jnp.concatenate([m_ref[b, r, 0:8] for b in quarters], axis=0)
+    cols = jnp.concatenate([m_ref[b, r, 8:16] for b in quarters], axis=0).astype(F32)
+    turned = pltpu.roll(cols, 64, 1)
+    zero = jnp.zeros((32, 128), F32)
+    first = jnp.concatenate([jnp.where(low, cols, zero), jnp.where(low, turned, zero)], 0)
+    second = jnp.concatenate([jnp.where(low, zero, turned), jnp.where(low, zero, cols)], 0)
+    first, second = first.astype(BF), second.astype(BF)
+    blank = jnp.zeros((64, 128), BF)
+    right = jnp.concatenate(
+        [
+            jnp.concatenate([first, blank], 1),
+            jnp.concatenate([blank, first], 1),
+            jnp.concatenate([second, blank], 1),
+            jnp.concatenate([blank, second], 1),
+        ],
+        0,
+    )
+    left = jnp.concatenate(
+        [
+            jnp.concatenate([planes[0], planes[1]], 1),
+            jnp.concatenate([planes[2], planes[3]], 1),
+            jnp.concatenate([weight, weight], 1),
+        ],
+        0,
+    )
+    half = lax.dot_general(
+        left, right, (((1,), (1,)), ((), ())), preferred_element_type=F32
+    ).astype(BF)
+    stacked = jnp.concatenate(
+        [
+            jnp.concatenate([half[p * 32 : p * 32 + 32, 0:128] for p in range(3)], 1),
+            jnp.concatenate([half[p * 32 : p * 32 + 32, 128:256] for p in range(3)], 1),
+        ],
+        0,
+    )
+    spread = jnp.dot(rows, q_ref[...], preferred_element_type=F32).astype(BF)
+    row_matrix = jnp.concatenate([spread[:, 0:64], spread[:, 128:192]], 0)
+    moved = jnp.dot(row_matrix, stacked, preferred_element_type=F32).astype(BF).astype(F32)
+    y_ref[slot] = moved[:, 0:256]
+    wt_ref[slot] = moved[:, 256:384] * present
+
+
+def robust_merge(y_ref, wt_ref, field_ref, u_ref, v_ref):
+    slots = y_ref.shape[0]
+    chunk = 16
+
+    def merge_rows(i, carry):
+        here = pl.ds(pl.multiple_of(i * chunk, chunk), chunk)
+
+        def load(n):
+            w = wt_ref[n, here, :]
+            return y_ref[n, here, :], jnp.concatenate([w, w], 1)
+
+        def plain(n, sums):
+            y, w = load(n)
+            return sums[0] + w * y, sums[1] + w
+
+        def robust(estimate, n, sums):
+            y, w = load(n)
+            size = jnp.maximum(jnp.abs(y - estimate), huber_delta)
+            h = w * pl.reciprocal(size, approx=True)
+            return sums[0] + h * y, sums[1] + h
+
+        empty = (jnp.zeros((chunk, 256), F32), jnp.zeros((chunk, 256), F32))
+        top, bottom = lax.fori_loop(0, slots, plain, empty, unroll=4)
+        estimate = top / (bottom + prior_weight)
+        for _ in range(HUBER_ITERS):
+            top, bottom = lax.fori_loop(
+                0, slots, functools.partial(robust, estimate), empty, unroll=4
+            )
+            estimate = top / (bottom + prior_weight / huber_delta)
+        field_ref[here, :] = estimate
+        return carry
+
+    lax.fori_loop(0, 64 // chunk, merge_rows, 0)
+    exact = lax.Precision.HIGHEST
+    ordered = jnp.dot(u_ref[...], field_ref[...], precision=exact, preferred_element_type=F32)
+    for pair in range(2):
+        here = slice(pair * 128, pair * 128 + 128)
+        field_ref[:, here] = jnp.dot(
+            ordered[:, here], v_ref[...], precision=exact, preferred_element_type=F32
+        )
+
+
+def order_matrices():
+    q = np.zeros((128, 256), np.float32)
+    u = np.zeros((64, 64), np.float32)
+    v = np.zeros((128, 128), np.float32)
+    for n in range(64):
+        place = (n % 2) * 32 + n // 2
+        q[n, place] = 1
+        q[64 + n, 128 + place] = 1
+        u[n, place] = 1
+        v[place, n] = 1
+        v[64 + place, 64 + n] = 1
+    return jnp.asarray(q, BF), jnp.asarray(u), jnp.asarray(v)
 
 
 MESH = pl.DeviceIdType.MESH
@@ -31,12 +137,26 @@
     w_in_ref,
     w_hid_ref,
     w_out_ref,
+    q_ref,
+    u_ref,
+    v_ref,
+    out_ref,
     planes_ref,
     weights_ref,
     matrices_ref,
     codes_ref,
     x_ref,
     own_ref,
+    stage_x,
+    stage_w,
+    stage_m,
+    stage_code,
+    y_ref,
+    wt_ref,
+    field_ref,
+    near_left,
+    near_right,
+    last_ref,
     local_sems,
     x_send,
     x_recv,
@@ -53,6 +173,8 @@
     mat_band_recv,
     weight_band_send,
     weight_band_recv,
+    halo_send,
+    halo_recv,
 ):
     tiles = planes_ref.shape[0]
     bands = quarters_ref.shape[0]
@@ -248,13 +370,131 @@
         forward(steps)
         steps += 1
     for_tiles(1, share_weights)
-    for_tiles(steps, forward)
-
     plane_local.wait()
     code_local.wait()
+    for_tiles(1, lambda k: code_copy(tile, tile_source(k)).wait_recv())
+    for k in range(1, bands):
+        peer = band_peer(k)
+        for ref, send, recv in (
+            (matrices_ref, mat_band_send, mat_band_recv),
+            (weights_ref, weight_band_send, weight_band_recv),
+        ):
+            whole = remote(ref.at[peer], ref.at[peer], send.at[peer], recv.at[peer], {"band": peer})
+            whole.wait_recv()
+
+    def reproject(first, last):
+        def turn(n, carry):
+            source = tile + (n // 2) * (1 - 2 * (n % 2))
+
+            @pl.when((source >= 0) & (source < tiles) & (n != 1))
+            def _():
+                copies = [
+                    pltpu.make_async_copy(planes_ref.at[source], stage_x, local_sems.at[5]),
+                    pltpu.make_async_copy(codes_ref.at[source], stage_code, local_sems.at[6]),
+                ]
+                for b in range(bands):
+                    copies.append(
+                        pltpu.make_async_copy(
+                            weights_ref.at[b, source], stage_w.at[b], local_sems.at[7 + 2 * b]
+                        )
+                    )
+                    copies.append(
+                        pltpu.make_async_copy(
+                            matrices_ref.at[b, source], stage_m.at[b], local_sems.at[8 + 2 * b]
+                        )
+                    )
+                for copy in copies:
+                    copy.start()
+                for copy in copies:
+                    copy.wait()
+                for r in range(cap):
+                    reproject_slot(
+                        r, source * cap + r, stage_code, stage_x, stage_w, stage_m, q_ref, y_ref,
+                        wt_ref,
+                    )
+
+            return carry
+
+        lax.fori_loop(2 * first, 2 * last, turn, 0)
+
+    if tiles <= 8:
+        begun = 0
+        for s in range(3, tiles, 3):
+            reproject(begun, s)
+            begun = s
+            if steps < tiles:
+                forward(steps)
+                steps += 1
+        for_tiles(steps, forward)
+        reproject(begun, tiles)
+    else:
+        for_tiles(steps, forward)
+        reproject(0, tiles)
+
+    robust_merge(y_ref, wt_ref, field_ref, u_ref, v_ref)
+
+    def halo(target, landing, way):
+        return remote(
+            field_ref, landing, halo_send.at[way], halo_recv.at[way], {"tile": target}
+        )
+
+    @pl.when(tile < tiles - 1)
+    def _():
+        halo(tile + 1, near_left, 0).start()
+
+    @pl.when(tile > 0)
+    def _():
+        halo(tile - 1, near_right, 1).start()
+
+    @pl.when(tile == 0)
+    def _():
+        near_left[...] = jnp.zeros_like(near_left)
+
+    @pl.when(tile == tiles - 1)
+    def _():
+        near_right[...] = jnp.zeros_like(near_right)
+
+    @pl.when(tile > 0)
+    def _():
+        halo(tile, near_left, 0).wait_recv()
+
+    @pl.when(tile < tiles - 1)
+    def _():
+        halo(tile, near_right, 1).wait_recv()
+
+    lane = lax.broadcasted_iota(jnp.int32, (64, 128), 1)
+    line = lax.broadcasted_iota(jnp.int32, (64, 128), 0)
+    shut = ((lane == 127) & (tile == 0)) | ((lane == 63) & (tile == tiles - 1))
+    for c in range(out_ref.shape[0]):
+        pair = pl.ds((c // 2) * 128, 128)
+        own, low, high = field_ref[:, pair], near_left[:, pair], near_right[:, pair]
+        if c % 2 == 0:
+            low, high = pltpu.roll(low, 64, 1), pltpu.roll(high, 64, 1)
+        else:
+            own = pltpu.roll(own, 64, 1)
+        g = jnp.where(lane < 64, own, jnp.where(lane < 96, high, low))
+        for _ in range(SMOOTH):
+            across = pltpu.roll(g, 127, 1) - g
+            side = jnp.where(shut, 0.0, across / (1.0 + across * across))
+            down = pltpu.roll(g, 63, 0) - g
+            upright = jnp.where(line == 63, 0.0, down / (1.0 + down * down))
+            g = g + smooth_rate * (
+                side - pltpu.roll(side, 1, 1) + (upright - pltpu.roll(upright, 1, 0))
+            )
+        last_ref[c] = g
+        even = last_ref[c, pl.ds(0, 32, stride=2), :]
+        odd = last_ref[c, pl.ds(1, 32, stride=2), :]
+        out_ref[c] = jnp.where(lane[:32] < 64, even, pltpu.roll(odd, 64, 1))
+
+    @pl.when(tile < tiles - 1)
+    def _():
+        halo(tile + 1, near_left, 0).wait_send()
+
+    @pl.when(tile > 0)
+    def _():
+        halo(tile - 1, near_right, 1).wait_send()
 
     def finish(k):
-        code_copy(tile, tile_source(k)).wait_recv()
         code_copy(tile_peer(k), tile).wait_send()
         mat_copy(tile_peer(k), tile).wait_send()
         weight_copy(tile_peer(k), tile).wait_send()
@@ -280,7 +520,6 @@
         ):
             whole = remote(ref.at[peer], ref.at[peer], send.at[peer], recv.at[peer], {"band": peer})
             whole.wait_send()
-            whole.wait_recv()
 
 
 def exchange(quarters, laid, sent, meta, scale, w_in, w_hidden, w_out):
@@ -299,9 +538,10 @@
     dma = pltpu.SemaphoreType.DMA
     return pl.pallas_call(
         functools.partial(exchange_kernel, max(1, scenes // 4)),
-        in_specs=[anywhere] * 4 + [vmem] * 4,
-        out_specs=[anywhere] * 4,
+        in_specs=[anywhere] * 4 + [vmem] * 7,
+        out_specs=[vmem] + [anywhere] * 4,
         out_shape=[
+            jax.ShapeDtypeStruct(laid.shape[1:], F32),
             jax.ShapeDtypeStruct((tiles,) + laid.shape, BF),
             jax.ShapeDtypeStruct((bands, tiles, scenes, lines, 128), BF),
             jax.ShapeDtypeStruct((bands, tiles, cap) + sent.shape[1:], BF),
@@ -310,175 +550,27 @@
         scratch_shapes=[
             pltpu.VMEM(quarters.shape, BF),
             pltpu.VMEM((scenes, lines, 128), BF),
-            dma((5,)),
+            pltpu.VMEM(laid.shape, BF),
+            pltpu.VMEM((bands, scenes, lines, 128), BF),
+            pltpu.VMEM((bands, cap) + sent.shape[1:], BF),
+            pltpu.SMEM(meta.shape[1:], jnp.int32),
+            pltpu.VMEM((tiles * cap, 64, 256), F32),
+            pltpu.VMEM((tiles * cap, 64, 128), F32),
+            pltpu.VMEM((64, 256), F32),
+            pltpu.VMEM((64, 256), F32),
+            pltpu.VMEM((64, 256), F32),
+            pltpu.VMEM((part, 64, 128), F32),
+            dma((7 + 2 * bands,)),
             dma((bands,)),
             dma((bands,)),
         ]
         + [dma((tiles,))] * 9
-        + [dma((bands,))] * 4,
+        + [dma((bands,))] * 4
+        + [dma((2,))] * 2,
         compiler_params=pltpu.CompilerParams(
             collective_id=0, has_side_effects=True, vmem_limit_bytes=32 * 1024 * 1024
         ),
-    )(quarters, laid, sent, meta, scale, w_in_t, w_hid_t, w_out_t)
-
-
-def merge_kernel(
-    cap, code_ref, x_ref, w_ref, m_ref, q_ref, u_ref, v_ref, out_ref, y_ref, wt_ref
-):
-    source = pl.program_id(0)
-    lane = lax.broadcasted_iota(jnp.int32, (32, 128), 1)
-    low = lane < 64
-    quarters = range(m_ref.shape[0])
-    for r in range(cap):
-        slot = source * cap + r
-        code = code_ref[slot]
-        scene = jnp.maximum(code, 0)
-        planes = x_ref[0, scene]
-        weight = jnp.concatenate([w_ref[b, 0, scene] for b in quarters], axis=0)
-        rows = jnp.concatenate([m_ref[b, 0, r, 0:8] for b in quarters], axis=0)
-        cols = jnp.concatenate([m_ref[b, 0, r, 8:16] for b in quarters], axis=0).astype(F32)
-        turned = pltpu.roll(cols, 64, 1)
-        zero = jnp.zeros((32, 128), F32)
-        first = jnp.concatenate([jnp.where(low, cols, zero), jnp.where(low, turned, zero)], 0)
-        second = jnp.concatenate([jnp.where(low, zero, turned), jnp.where(low, zero, cols)], 0)
-        first, second = first.astype(BF), second.astype(BF)
-        blank = jnp.zeros((64, 128), BF)
-        right = jnp.concatenate(
-            [
-                jnp.concatenate([first, blank], 1),
-                jnp.concatenate([blank, first], 1),
-                jnp.concatenate([second, blank], 1),
-                jnp.concatenate([blank, second], 1),
-            ],
-            0,
-        )
-        left = jnp.concatenate(
-            [
-                jnp.concatenate([planes[0], planes[1]], 1),
-                jnp.concatenate([planes[2], planes[3]], 1),
-                jnp.concatenate([weight, weight], 1),
-            ],
-            0,
-        )
-        half = lax.dot_general(
-            left, right, (((1,), (1,)), ((), ())), preferred_element_type=F32
-        ).astype(BF)
-        stacked = jnp.concatenate(
-            [
-                jnp.concatenate([half[p * 32 : p * 32 + 32, 0:128] for p in range(3)], 1),
-                jnp.concatenate([half[p * 32 : p * 32 + 32, 128:256] for p in range(3)], 1),
-            ],
-            0,
-        )
-        spread = jnp.dot(rows, q_ref[...], preferred_element_type=F32).astype(BF)
-        row_matrix = jnp.concatenate([spread[:, 0:64], spread[:, 128:192]], 0)
-        moved = jnp.dot(row_matrix, stacked, preferred_element_type=F32)
-        present = jnp.where(code >= 0, 1.0, 0.0)
-        y_ref[slot] = moved[:, 0:256].astype(BF)
-        wt_ref[slot] = (moved[:, 256:384] * present).astype(BF)
-
-    @pl.when(source == pl.num_programs(0) - 1)
-    def _():
-        slots = y_ref.shape[0]
-        chunk = 16
-
-        def merge_rows(i, carry):
-            here = pl.ds(pl.multiple_of(i * chunk, chunk), chunk)
-
-            def load(n):
-                y = y_ref[n, here, :].astype(F32)
-                w = wt_ref[n, here, :].astype(F32)
-                return y, jnp.concatenate([w, w], 1)
-
-            def plain(n, sums):
-                y, w = load(n)
-                return sums[0] + w * y, sums[1] + w
-
-            def robust(estimate, n, sums):
-                y, w = load(n)
-                size = jnp.maximum(jnp.abs(y - estimate), huber_delta)
-                h = w * (huber_delta * pl.reciprocal(size, approx=True))
-                return sums[0] + h * y, sums[1] + h
-
-            empty = (jnp.zeros((chunk, 256), F32), jnp.zeros((chunk, 256), F32))
-            top, bottom = lax.fori_loop(0, slots, plain, empty, unroll=4)
-            estimate = top / (bottom + prior_weight)
-            for _ in range(HUBER_ITERS):
-                top, bottom = lax.fori_loop(
-                    0, slots, functools.partial(robust, estimate), empty, unroll=4
-                )
-                estimate = top / (bottom + prior_weight)
-            out_ref[here, :] = estimate
-            return carry
-
-        lax.fori_loop(0, 64 // chunk, merge_rows, 0)
-        exact = lax.Precision.HIGHEST
-        ordered = jnp.dot(u_ref[...], out_ref[...], precision=exact, preferred_element_type=F32)
-        out_ref[:, 0:128] = jnp.dot(
-            ordered[:, 0:128], v_ref[...], precision=exact, preferred_element_type=F32
-        )
-        out_ref[:, 128:256] = jnp.dot(
-            ordered[:, 128:256], v_ref[...], precision=exact, preferred_element_type=F32
-        )
-
-
-def order_matrices():
-    q = np.zeros((128, 256), np.float32)
-    u = np.zeros((64, 64), np.float32)
-    v = np.zeros((128, 128), np.float32)
-    for n in range(64):
-        place = (n % 2) * 32 + n // 2
-        q[n, place] = 1
-        q[64 + n, 128 + place] = 1
-        u[n, place] = 1
-        v[place, n] = 1
-        v[64 + place, 64 + n] = 1
-    return jnp.asarray(q, BF), jnp.asarray(u), jnp.asarray(v)
-
-
-def merge(codes, planes, weights, matrices):
-    quarters, sources, scenes, lines, _ = weights.shape
-    cap = matrices.shape[2]
-    slots = sources * cap
-    q, u, v = order_matrices()
-    return pl.pallas_call(
-        functools.partial(merge_kernel, cap),
-        grid_spec=pltpu.PrefetchScalarGridSpec(
-            num_scalar_prefetch=1,
-            grid=(sources,),
-            in_specs=[
-                pl.BlockSpec((1, scenes, 4, 32, 128), lambda d, *_: (d, 0, 0, 0, 0)),
-                pl.BlockSpec((quarters, 1, scenes, lines, 128), lambda d, *_: (0, d, 0, 0, 0)),
-                pl.BlockSpec((quarters, 1, cap, 16, 128), lambda d, *_: (0, d, 0, 0, 0)),
-                pl.BlockSpec((128, 256), lambda d, *_: (0, 0)),
-                pl.BlockSpec((64, 64), lambda d, *_: (0, 0)),
-                pl.BlockSpec((128, 128), lambda d, *_: (0, 0)),
-            ],
-            out_specs=pl.BlockSpec((64, 256), lambda d, *_: (0, 0)),
-            scratch_shapes=[
-                pltpu.VMEM((slots, 64, 256), BF),
-                pltpu.VMEM((slots, 64, 128), BF),
-            ],
-        ),
-        out_shape=jax.ShapeDtypeStruct((64, 256), F32),
-        compiler_params=pltpu.CompilerParams(vmem_limit_bytes=40 * 1024 * 1024),
-        cost_estimate=pl.CostEstimate(
-            flops=slots * 40_000_000, bytes_accessed=8 * 1024 * 1024, transcendentals=slots * 65536
-        ),
-    )(codes, planes, weights, matrices, q, u, v)
-
-
-def smooth_step(extended, first_col, total_cols):
-    positions = first_col + jnp.arange(extended.shape[2] - 1)
-    inside = ((positions >= 0) & (positions + 1 < total_cols)).astype(F32)
-    across = extended[:, :, 1:] - extended[:, :, :-1]
-    sideways = across / (1.0 + (across / edge_scale) ** 2) * inside
-    centre = extended[:, :, 1:-1]
-    upward_diff = centre[:, 1:, :] - centre[:, :-1, :]
-    upward = upward_diff / (1.0 + (upward_diff / edge_scale) ** 2)
-    zeros_row = jnp.zeros_like(upward[:, :1, :])
-    vertical = jnp.concatenate([upward, zeros_row], 1) - jnp.concatenate([zeros_row, upward], 1)
-    return centre + smooth_rate * (sideways[:, :, 1:] - sideways[:, :, :-1] + vertical)
+    )(quarters, laid, sent, meta, scale, w_in_t, w_hid_t, w_out_t, *order_matrices())[0]
 
 
 def per_device(
@@ -528,20 +620,7 @@
     )
     sent = jnp.dot(pick, both, preferred_element_type=F32).astype(BF)
     sent = sent.reshape(tile_count * cap, 2 * part // 128, 128)
-    planes, weights, matrices, codes = exchange(
-        quarters, laid, sent, meta, scale, w_in, w_hidden, w_out
-    )
-    estimate = merge(codes[:, 0, :cap].reshape(-1), planes, weights, matrices)
-    field = estimate.reshape(side_cells, group_bands, side_cells).transpose(1, 0, 2)
-
-    forward = [(i, i + 1) for i in range(tile_count - 1)]
-    backward = [(i + 1, i) for i in range(tile_count - 1)]
-    low = lax.ppermute(field[:, :, side_cells - SMOOTH :], "tile", forward)
-    high = lax.ppermute(field[:, :, :SMOOTH], "tile", backward)
-    field = jnp.concatenate([low, field, high], 2)
-    for step in range(SMOOTH):
-        first_col = tile * side_cells - SMOOTH + step
-        field = smooth_step(field, first_col, tile_count * side_cells)
+    field = exchange(quarters, laid, sent, meta, scale, w_in, w_hidden, w_out)
     return field.reshape(group_bands, pixel_count)
 
 

time: 109 us -> 105 us (0.963)
  Pallas kernels: 83.1 us -> 95 us
  local copies, waits for them, and re-layouts: 12.4 us -> 5.63 us
  starting transfers between devices: 5.37 us -> 0 us
  waiting for transfers between devices: 4.32 us -> 0 us
    pallas_call x1, Pallas kernels: 56.6 us -> 95 us  [exchange(): pl.pallas_call(functools.partial(exchange_kernel, max(1, scenes // 4)), i...]
    pallas_call x1 -> x0, Pallas kernels: 26.5 us -> none  [merge(): pl.pallas_call(functools.partial(merge_kernel, cap), grid_spec=pltpu.Pref...]
    ppermute x2 -> x0, starting transfers between devices: 5.37 us -> none  [the longest x1 3.45 us: per_device(): low = lax.ppermute(field[:, :, side_cells - SMOOTH:], 'tile', forward)]
    ppermute x2 -> x0, waiting for transfers between devices: 4.32 us -> none  [the longest x1 4.31 us: per_device(): high = lax.ppermute(field[:, :, :SMOOTH], 'tile', backward)]
    unnamed x23 -> x12, local copies, waits for them, and re-layouts: 6.68 us -> 2.58 us
    another operation x1, local copies, waits for them, and re-layouts: 1.38 us -> 0.2 us  [per_device(): jnp.stack([granules[:, :, b * part:(b + 1) * part] for b in range(band_co...]
  transfers between devices with their start and end apart: 2 -> 0, of which waited for: 1 -> 0; matrix products, arithmetic and copies ran while one was open for 0% -> 0% of each run, Pallas kernels for 0% -> 0%
where the time goes in v3:
time: 105 us; the launch traced here: 104 us
  Pallas kernels  95 us (90%)
  local copies, waits for them, and re-layouts  5.63 us (5%)
  other arithmetic  3.15 us (3%)
    pallas_call x1, Pallas kernels, exchange(): pl.pallas_call(functools.partial(exchange_kernel, max(1, scenes // 4)), i...  95 us
    unnamed x12, local copies, waits for them, and re-layouts  2.58 us

profile of v3, /device:TPU:1, one launch (start us, length us, event | category | flops | bytes accessed | tf_op | source)
XLA Modules:
  0.0 104.3 jit_solution(10948827834444806376)
XLA Ops:
  0.0 0.0 copy-start
  0.0 0.0 copy-start.2
  0.0 0.0 copy-start.1
  0.0 0.0 copy-start.3
  0.0 0.7 add_exponential_fusion
  0.8 0.1 eq.54
  0.8 0.8 convert_multiply_fusion
  1.6 0.8 copy.23
  2.4 0.1 eq.47
  2.5 0.2 reduce_window_sum.11
  2.7 0.2 select_reduce_fusion
  2.9 0.7 broadcast_multiply_fusion
  3.6 0.7 broadcast_in_dim.19.w_out_ref
  4.3 0.1 copy.25
  4.5 0.1 broadcast_in_dim.14
  4.6 0.1 reshape.130.scale_ref
  4.7 1.1 %constant_dynamic-slice_fusion = (bf16[16,4,1024]{2,1,0:T(4,128)(2,1)S(1)}, bf16[16,4,1024]{2,1,0:T(4,128)(2,1)S(1)}) fusion(bf16[16,4,4096]{2,1,0:T(4,128)(2,1)} %param.19, s32[]{:T(128)S(6)} %select_n.20, bf16[16,4,4096]{2,1,0:T(4,128)(2,1)} %param.18), kind=kLoop, calls=%fused_computation.27 | loop fusion | bytes 524292 | tf_op jit(solution)/shard_map/dynamic_slice | solution.py:616
  5.8 0.3 fusion
  6.2 1.1 %copy.26 = bf16[2,256,256]{1,2,0:T(8,128)(2,1)S(1)} copy(bf16[2,256,256]{2,1,0:T(8,128)(2,1)} %param.21) | data formatting | bytes 524288 | tf_op args[7]
  7.3 0.0 copy-done.3
  7.3 0.5 reshape.126.laid_ref
  7.8 0.2 slice_bitcast_fusion.3
  8.1 0.5 pad_maximum_fusion.quarters_ref
  8.5 0.0 copy-done
  8.5 0.0 copy-done.2
  8.5 0.0 copy-done.1
  8.6 95.0 %shard_map.118 = (f32[4,32,128]{2,1,0:T(8,128)S(1)}, bf16[8,16,4,32,128]{4,3,2,1,0:T(8,128)(2,1)}, bf16[4,8,16,8,128]{4,3,2,1,0:T(8,128)(2,1)}, bf16[4,8,9,16,128]{4,3,2,1,0:T(8,128)(2,1)}, s32[8,8,128]{2,1,0:T(8,128)}) custom-call(bf16[4,16,4,1024]{3,2,1,0:T(4,128)(2,1)S(1)} %pad_maximum_fusion.quarters_ref, ...), custom_call_target="tpu_custom_call" | custom-call | tf_op jit(solution)/shard_map/pallas_call | solution.py:539
  103.6 0.7 copy.30
  (14 shorter events, 0.2 us)
Async XLA Ops:
  0.0 8.5 %copy-start = (f32[128,128]{1,0:T(8,128)S(1)}, f32[128,128]{1,0:T(8,128)}, u32[]{:S(2)}) copy-start(f32[128,128]{1,0:T(8,128)} %constant.88.clone.v_ref) | copy-start | bytes 196612
  0.0 8.5 %copy-start.2 = (f32[64,64]{1,0:T(8,128)S(1)}, f32[64,64]{1,0:T(8,128)}, u32[]{:S(2)}) copy-start(f32[64,64]{1,0:T(8,128)} %constant.87.clone.u_ref) | copy-start | bytes 49156
  0.0 8.5 %copy-start.1 = (bf16[128,256]{1,0:T(8,128)(2,1)S(1)}, bf16[128,256]{1,0:T(8,128)(2,1)}, u32[]{:S(2)}) copy-start(bf16[128,256]{1,0:T(8,128)(2,1)} %constant.86.clone.q_ref) | copy-start | bytes 196612
  0.0 7.3 %copy-start.3 = (bf16[16,4,4096]{2,1,0:T(4,128)(2,1)S(1)}, bf16[16,4,4096]{2,1,0:T(4,128)(2,1)}, u32[]{:S(2)}) copy-start(bf16[16,4,4096]{2,1,0:T(4,128)(2,1)} %param.14) | copy-start | bytes 1572868

commit v4 on v3

--- a/solution.py
+++ b/solution.py
@@ -128,15 +128,15 @@
 
 
 def exchange_kernel(
-    segment,
     quarters_ref,
     laid_ref,
     sent_ref,
     meta_ref,
-    scale_ref,
-    w_in_ref,
-    w_hid_ref,
-    w_out_ref,
+    valid_ref,
+    order_ref,
+    w_in_raw,
+    w_hid_raw,
+    w_out_raw,
     q_ref,
     u_ref,
     v_ref,
@@ -147,6 +147,8 @@
     codes_ref,
     x_ref,
     own_ref,
+    w_in_ref,
+    w_hid_ref,
     stage_x,
     stage_w,
     stage_m,
@@ -297,21 +299,20 @@
     def forward(s):
         left, right = tile - s, tile + s
 
-        @pl.when(left >= 0)
+        @pl.when((left >= 0) & (tile < tiles - 1))
         def _():
             plane_copy(left, tile, right_send).wait_recv()
-
-            @pl.when(tile < tiles - 1)
-            def _():
-                plane_copy(left, tile + 1, right_send).start()
-
-        @pl.when(right < tiles)
+            plane_copy(left, tile + 1, right_send).start()
+
+        @pl.when((right < tiles) & (tile > 0))
         def _():
             plane_copy(right, tile, left_send).wait_recv()
-
-            @pl.when(tile > 0)
-            def _():
-                plane_copy(right, tile - 1, left_send).start()
+            plane_copy(right, tile - 1, left_send).start()
+
+    def arrive(source):
+        @pl.when((tile == 0) | (tile == tiles - 1))
+        def _():
+            plane_copy(source, tile, right_send).wait_recv()
 
     def network(scene, carry):
         def silu(t):
@@ -321,10 +322,21 @@
         hidden = silu(jnp.dot(w_in_ref[...], x, preferred_element_type=F32))
         for layer in range(w_hid_ref.shape[0]):
             hidden = silu(jnp.dot(w_hid_ref[layer], hidden, preferred_element_type=F32))
-        logits = jnp.dot(w_out_ref[...], hidden, preferred_element_type=F32)
+        w_out = jnp.broadcast_to(w_out_raw[...].astype(F32), (16, w_out_raw.shape[1]))
+        logits = jnp.dot(w_out.astype(BF), hidden, preferred_element_type=F32)
         row = jax.nn.sigmoid(-logits[0:1])
         pieces = [row[:, i * 128 : (i + 1) * 128] for i in range(row.shape[1] // 128)]
-        own_ref[scene] = (jnp.concatenate(pieces, axis=0) * scale_ref[scene]).astype(BF)
+        shape = (len(pieces), 128)
+        line = lax.broadcasted_iota(jnp.int32, shape, 0)
+        lane = lax.broadcasted_iota(jnp.int32, shape, 1)
+        valid = jnp.zeros(shape, F32)
+        side = 2 * len(pieces)
+        for i in range(side):
+            here = (line == i // 2) & (lane // 64 == i % 2)
+            valid = jnp.where(here, valid_ref[scene, band * side + i].astype(F32), valid)
+        order = jnp.full(shape, order_ref[scene], jnp.int32).astype(F32)
+        recency = jnp.exp(1.4 * order / (scenes * tiles) - 0.7)
+        own_ref[scene] = (jnp.concatenate(pieces, axis=0) * valid * recency).astype(BF)
         return carry
 
     def share_matrices():
@@ -340,18 +352,21 @@
 
         for_tiles(1, share)
 
+    w_in_ref[...] = (w_in_raw[...].astype(F32) * 0.5).T.astype(BF)
+    for layer in range(w_hid_raw.shape[0]):
+        w_hid_ref[layer] = (w_hid_raw[layer].astype(F32) * 0.5).T.astype(BF)
     for k in range(1, bands):
         source = lax.rem(band + bands - k, bands)
         x_copy(source, source).wait_recv()
     x_local.wait()
     steps = 1
-    for start in range(0, scenes, segment):
-        lax.fori_loop(start, start + segment, network, 0)
-        if steps < tiles:
+    for first, last in ((0, 3), (3, 7), (7, 13), (13, 16)):
+        if steps < min(4, tiles):
             forward(steps)
             steps += 1
-        if start == 2 * segment:
+        if first == 7:
             share_matrices()
+        lax.fori_loop(first * scenes // 16, last * scenes // 16, network, 0)
 
     weight_local = pltpu.make_async_copy(own_ref, weights_ref.at[band, tile], local_sems.at[4])
     weight_local.start()
@@ -370,6 +385,9 @@
         forward(steps)
         steps += 1
     for_tiles(1, share_weights)
+    if steps < tiles:
+        forward(steps)
+        steps += 1
     plane_local.wait()
     code_local.wait()
     for_tiles(1, lambda k: code_copy(tile, tile_source(k)).wait_recv())
@@ -388,6 +406,10 @@
 
             @pl.when((source >= 0) & (source < tiles) & (n != 1))
             def _():
+                @pl.when(n > 0)
+                def _():
+                    arrive(source)
+
                 copies = [
                     pltpu.make_async_copy(planes_ref.at[source], stage_x, local_sems.at[5]),
                     pltpu.make_async_copy(codes_ref.at[source], stage_code, local_sems.at[6]),
@@ -522,23 +544,20 @@
             whole.wait_send()
 
 
-def exchange(quarters, laid, sent, meta, scale, w_in, w_hidden, w_out):
+def exchange(quarters, laid, sent, meta, valid_rows, scene_order, w_in, w_hidden, w_out):
     bands, scenes, part, width = quarters.shape
     tiles = meta.shape[0]
     cap = sent.shape[0] // tiles
     hid = w_in.shape[1]
     layers = w_hidden.shape[0]
-    half = jnp.asarray(0.5, BF)
-    w_in_t = (w_in * half).T
-    w_hid_t = jnp.swapaxes(w_hidden * half, 1, 2)
-    w_out_t = jnp.broadcast_to(w_out[None, :], (16, hid))
     lines = width // 128
     anywhere = pl.BlockSpec(memory_space=pl.ANY)
     vmem = pl.BlockSpec(memory_space=pltpu.VMEM)
+    smem = pl.BlockSpec(memory_space=pltpu.SMEM)
     dma = pltpu.SemaphoreType.DMA
     return pl.pallas_call(
-        functools.partial(exchange_kernel, max(1, scenes // 4)),
-        in_specs=[anywhere] * 4 + [vmem] * 7,
+        exchange_kernel,
+        in_specs=[anywhere] * 4 + [smem] * 2 + [vmem] * 6,
         out_specs=[vmem] + [anywhere] * 4,
         out_shape=[
             jax.ShapeDtypeStruct(laid.shape[1:], F32),
@@ -550,6 +569,8 @@
         scratch_shapes=[
             pltpu.VMEM(quarters.shape, BF),
             pltpu.VMEM((scenes, lines, 128), BF),
+            pltpu.VMEM((hid, bands * part), BF),
+            pltpu.VMEM((layers, hid, hid), BF),
             pltpu.VMEM(laid.shape, BF),
             pltpu.VMEM((bands, scenes, lines, 128), BF),
             pltpu.VMEM((bands, cap) + sent.shape[1:], BF),
@@ -570,7 +591,10 @@
         compiler_params=pltpu.CompilerParams(
             collective_id=0, has_side_effects=True, vmem_limit_bytes=32 * 1024 * 1024
         ),
-    )(quarters, laid, sent, meta, scale, w_in_t, w_hid_t, w_out_t, *order_matrices())[0]
+    )(
+        quarters, laid, sent, meta, valid_rows, scene_order, w_in, w_hidden, w_out[None, :],
+        *order_matrices(),
+    )[0]
 
 
 def per_device(
@@ -585,7 +609,6 @@
     w_out,
 ):
     scenes, group_bands, pixel_count = granules.shape
-    side_cells = valid_rows.shape[1]
     top = intersections.shape[1]
     tile_count = lax.axis_size("tile")
     band_count = lax.axis_size("band")
@@ -594,15 +617,9 @@
     entry_count = scenes * top
     cap = (entry_count + tile_count - 1) // tile_count + 1
     part = pixel_count // band_count
-    row_count = side_cells // band_count
 
     laid = granules.reshape(scenes, group_bands, pixel_count // 128, 128)
     quarters = jnp.stack([granules[:, :, b * part : (b + 1) * part] for b in range(band_count)])
-    recency = jnp.exp(1.4 * scene_order.astype(F32) / (scenes * tile_count) - 0.7)
-    valid_here = lax.dynamic_slice_in_dim(valid_rows, band * row_count, row_count, 1).astype(F32)
-    scale = valid_here * recency[:, None]
-    scale = jnp.broadcast_to(scale[:, :, None], (scenes, row_count, side_cells))
-    scale = scale.reshape(scenes, part // 128, 128)
     flat_dest = intersections.reshape(entry_count)
     is_dest = flat_dest[None, :] == jnp.arange(tile_count, dtype=jnp.int32)[:, None]
     rank = jnp.cumsum(is_dest.astype(jnp.int32), 1) - 1
@@ -620,7 +637,9 @@
     )
     sent = jnp.dot(pick, both, preferred_element_type=F32).astype(BF)
     sent = sent.reshape(tile_count * cap, 2 * part // 128, 128)
-    field = exchange(quarters, laid, sent, meta, scale, w_in, w_hidden, w_out)
+    field = exchange(
+        quarters, laid, sent, meta, valid_rows, scene_order, w_in, w_hidden, w_out
+    )
     return field.reshape(group_bands, pixel_count)
 
 

time: 105 us -> 103 us (0.981)
  other arithmetic: 3.15 us -> 0.92 us
    mul x2 -> x0, other arithmetic: 1.48 us -> none  [the longest x1 0.77 us: per_device(): scale = valid_here * recency[:, None]]
    another operation x1, local copies, waits for them, and re-layouts: 0.2 us -> 1.29 us  [per_device(): jnp.stack([granules[:, :, b * part:(b + 1) * part] for b in range(band_co...]
    unnamed x12 -> x17, local copies, waits for them, and re-layouts: 2.58 us -> 1.51 us
where the time goes in v4:
time: 103 us; the launch traced here: 102 us
  Pallas kernels  94.5 us (92%)
  local copies, waits for them, and re-layouts  6.47 us (6%)
    pallas_call x1, Pallas kernels, exchange(): pl.pallas_call(exchange_kernel, in_specs=[anywhere] * 4 + [smem] * 2 + [v...  94.5 us

profile of v4, /device:TPU:1, one launch (start us, length us, event | category | flops | bytes accessed | tf_op | source)
XLA Modules:
  0.0 102.4 jit_solution(6683146661001661542)
XLA Ops:
  0.0 0.0 copy-start.1
  0.0 0.0 copy-start.3
  0.0 0.0 copy-start.2
  0.0 0.0 copy-start
  0.0 0.0 copy-start.5
  0.0 0.0 copy-start.6
  0.0 0.0 copy-start.4
  0.1 0.7 broadcast_in_dim.23.w_out_raw
  0.8 0.1 eq.54
  0.9 0.8 copy.15
  1.6 0.1 eq.47
  1.7 0.2 reduce_window_sum.11
  2.0 0.2 select_reduce_fusion
  2.3 1.1 %constant_dynamic-slice_fusion = (bf16[16,4,1024]{2,1,0:T(4,128)(2,1)S(1)}, bf16[16,4,1024]{2,1,0:T(4,128)(2,1)S(1)}) fusion(bf16[16,4,4096]{2,1,0:T(4,128)(2,1)} %param.19, s32[]{:T(128)S(6)} %select_n.17, bf16[16,4,4096]{2,1,0:T(4,128)(2,1)} %param.18), kind=kLoop, calls=%fused_computation.25 | loop fusion | bytes 524292 | tf_op jit(solution)/shard_map/dynamic_slice | solution.py:633
  3.4 0.3 fusion
  3.8 1.6 %reshape.120.laid_ref = bf16[16,4,32,128]{3,2,1,0:T(8,128)(2,1)S(1)} reshape(bf16[16,4,4096]{2,1,0:T(4,128)(2,1)} %param.14) | data formatting | bytes 1048576 | tf_op jit(solution)/shard_map/reshape | solution.py:621
  5.3 1.3 %slice_bitcast_fusion.3 = (bf16[1,16,4,1024]{3,2,1,0:T(4,128)(2,1)S(1)}, bf16[1,16,4,1024]{3,2,1,0:T(4,128)(2,1)S(1)}, bf16[1,16,4,1024]{3,2,1,0:T(4,128)(2,1)S(1)}, bf16[1,16,4,1024]{3,2,1,0:T(4,128)(2,1)S(1)}) fusion(bf16[16,4,4096]{2,1,0:T(4,128)(2,1)} %param.14), kind=kLoop, calls=%fused_computation.9 | loop fusion | bytes 1048576 | tf_op jit(solution)/shard_map/stack | solution.py:622
  6.6 0.5 pad_maximum_fusion.quarters_ref
  7.1 0.0 copy-done.1
  7.1 0.0 copy-done.3
  7.1 0.0 copy-done.2
  7.2 0.0 copy-done
  7.2 0.0 copy-done.5
  7.2 0.0 copy-done.6
  7.2 0.0 copy-done.4
  7.2 94.5 %shard_map.118 = (f32[4,32,128]{2,1,0:T(8,128)S(1)}, bf16[8,16,4,32,128]{4,3,2,1,0:T(8,128)(2,1)}, bf16[4,8,16,8,128]{4,3,2,1,0:T(8,128)(2,1)}, bf16[4,8,9,16,128]{4,3,2,1,0:T(8,128)(2,1)}, s32[8,8,128]{2,1,0:T(8,128)}) custom-call(bf16[4,16,4,1024]{3,2,1,0:T(4,128)(2,1)S(1)} %pad_maximum_fusion.quarters_ref, ...), custom_call_target="tpu_custom_call" | custom-call | tf_op jit(solution)/shard_map/pallas_call | solution.py:558
  101.7 0.7 copy.20
  (13 shorter events, 0.2 us)
Async XLA Ops:
  0.0 7.1 %copy-start.1 = (f32[128,128]{1,0:T(8,128)S(1)}, f32[128,128]{1,0:T(8,128)}, u32[]{:S(2)}) copy-start(f32[128,128]{1,0:T(8,128)} %constant.73.clone.v_ref) | copy-start | bytes 196612
  0.0 7.1 %copy-start.3 = (f32[64,64]{1,0:T(8,128)S(1)}, f32[64,64]{1,0:T(8,128)}, u32[]{:S(2)}) copy-start(f32[64,64]{1,0:T(8,128)} %constant.72.clone.u_ref) | copy-start | bytes 49156
  0.0 7.1 %copy-start.2 = (bf16[128,256]{1,0:T(8,128)(2,1)S(1)}, bf16[128,256]{1,0:T(8,128)(2,1)}, u32[]{:S(2)}) copy-start(bf16[128,256]{1,0:T(8,128)(2,1)} %constant.71.clone.q_ref) | copy-start | bytes 196612
  0.0 7.1 %copy-start = (bf16[2,256,256]{2,1,0:T(8,128)(2,1)S(1)}, bf16[2,256,256]{2,1,0:T(8,128)(2,1)}, u32[]{:S(2)}) copy-start(bf16[2,256,256]{2,1,0:T(8,128)(2,1)} %w_hid_raw.1) | copy-start | bytes 786436
  0.0 7.1 %copy-start.5 = (bf16[16,256]{1,0:T(8,128)(2,1)S(1)}, bf16[16,256]{1,0:T(8,128)(2,1)}, u32[]{:S(2)}) copy-start(bf16[16,256]{1,0:T(8,128)(2,1)} %w_in_raw.1) | copy-start | bytes 24580
  0.0 7.1 %copy-start.6 = (s32[16]{0:T(128)S(1)}, s32[16]{0:T(128)}, u32[]{:S(2)}) copy-start(s32[16]{0:T(128)} %order_ref.1) | copy-start | bytes 196
  0.0 7.1 %copy-start.4 = (s32[16,64]{1,0:T(8,128)S(1)}, s32[16,64]{1,0:T(8,128)}, u32[]{:S(2)}) copy-start(s32[16,64]{1,0:T(8,128)} %valid_ref.1) | copy-start | bytes 12292

commit v5 on v4

--- a/solution.py
+++ b/solution.py
@@ -17,17 +17,19 @@
 F32 = jnp.float32
 
 
-def reproject_slot(r, slot, code_ref, x_ref, w_ref, m_ref, q_ref, y_ref, wt_ref):
+def reproject_slot(r, cap, source, code_ref, x_ref, w_ref, m_ref, q_ref, y_ref, wt_ref):
+    slot = source * cap + r
+    side, place = lax.rem(source, 2), source // 2
     lane = lax.broadcasted_iota(jnp.int32, (32, 128), 1)
     low = lane < 64
     quarters = range(m_ref.shape[0])
-    code = code_ref[0, r]
+    code = code_ref[source, 0, r]
     scene = jnp.maximum(code, 0)
     present = jnp.minimum(code + 1, 1).astype(F32)
     planes = x_ref[scene]
-    weight = jnp.concatenate([w_ref[b, scene] for b in quarters], axis=0)
-    rows = jnp.concatenate([m_ref[b, r, 0:8] for b in quarters], axis=0)
-    cols = jnp.concatenate([m_ref[b, r, 8:16] for b in quarters], axis=0).astype(F32)
+    weight = jnp.concatenate([w_ref[b, side, place, scene] for b in quarters], axis=0)
+    rows = jnp.concatenate([m_ref[b, source, r, 0:8] for b in quarters], axis=0)
+    cols = jnp.concatenate([m_ref[b, source, r, 8:16] for b in quarters], axis=0).astype(F32)
     turned = pltpu.roll(cols, 64, 1)
     zero = jnp.zeros((32, 128), F32)
     first = jnp.concatenate([jnp.where(low, cols, zero), jnp.where(low, turned, zero)], 0)
@@ -142,16 +144,15 @@
     v_ref,
     out_ref,
     planes_ref,
+    codes_ref,
     weights_ref,
     matrices_ref,
-    codes_ref,
     x_ref,
     own_ref,
     w_in_ref,
     w_hid_ref,
-    stage_x,
-    stage_w,
-    stage_m,
+    stage_even,
+    stage_odd,
     stage_code,
     y_ref,
     wt_ref,
@@ -175,6 +176,8 @@
     mat_band_recv,
     weight_band_send,
     weight_band_recv,
+    twin_send,
+    twin_recv,
     halo_send,
     halo_recv,
 ):
@@ -251,10 +254,13 @@
             {"tile": peer},
         )
 
+    parity = lax.rem(tile, 2)
+    twin = tile + 1 - 2 * parity
+
     def weight_copy(peer, source):
         return remote(
-            own_ref, weights_ref.at[band, source], weight_send.at[peer], weight_recv.at[source],
-            {"tile": peer},
+            own_ref, weights_ref.at[band, parity, source // 2], weight_send.at[peer],
+            weight_recv.at[source], {"tile": peer},
         )
 
     def mat_band_copy(source, peer, owner):
@@ -264,10 +270,14 @@
         )
 
     def weight_band_copy(source, peer, owner):
-        return remote(
-            weights_ref.at[owner, source], weights_ref.at[owner, source],
-            weight_band_send.at[peer], weight_band_recv.at[owner], {"band": peer},
-        )
+        shard = weights_ref.at[owner, parity, source // 2]
+        return remote(
+            shard, shard, weight_band_send.at[peer], weight_band_recv.at[owner], {"band": peer}
+        )
+
+    def twin_copy(owner, side):
+        shard = weights_ref.at[owner, side]
+        return remote(shard, shard, twin_send.at[owner], twin_recv.at[owner], {"tile": twin})
 
     for k in range(1, bands):
         x_copy(band_peer(k), band).start()
@@ -308,11 +318,6 @@
         def _():
             plane_copy(right, tile, left_send).wait_recv()
             plane_copy(right, tile - 1, left_send).start()
-
-    def arrive(source):
-        @pl.when((tile == 0) | (tile == tiles - 1))
-        def _():
-            plane_copy(source, tile, right_send).wait_recv()
 
     def network(scene, carry):
         def silu(t):
@@ -368,9 +373,19 @@
             share_matrices()
         lax.fori_loop(first * scenes // 16, last * scenes // 16, network, 0)
 
-    weight_local = pltpu.make_async_copy(own_ref, weights_ref.at[band, tile], local_sems.at[4])
+    weight_local = pltpu.make_async_copy(
+        own_ref, weights_ref.at[band, parity, tile // 2], local_sems.at[4]
+    )
     weight_local.start()
-    for_tiles(1, lambda k: weight_copy(tile_peer(k), tile).start())
+
+    def for_same(body):
+        def step(k, carry):
+            body(2 * k)
+            return carry
+
+        lax.fori_loop(1, tiles // 2, step, 0)
+
+    for_same(lambda k: weight_copy(tile_peer(k), tile).start())
     weight_local.wait()
     for k in range(1, bands):
         weight_band_copy(tile, band_peer(k), band).start()
@@ -384,74 +399,87 @@
     if steps < tiles:
         forward(steps)
         steps += 1
-    for_tiles(1, share_weights)
+    for_same(share_weights)
+    twin_copy(band, parity).start()
     if steps < tiles:
         forward(steps)
         steps += 1
     plane_local.wait()
     code_local.wait()
     for_tiles(1, lambda k: code_copy(tile, tile_source(k)).wait_recv())
+    code_copies = pltpu.make_async_copy(codes_ref, stage_code, local_sems.at[4])
+    code_copies.start()
+
+    def mat_band_all(peer):
+        whole = matrices_ref.at[peer]
+        return remote(
+            whole, whole, mat_band_send.at[peer], mat_band_recv.at[peer], {"band": peer}
+        )
+
+    def weight_band_all(peer, side):
+        whole = weights_ref.at[peer, side]
+        return remote(
+            whole, whole, weight_band_send.at[peer], weight_band_recv.at[peer], {"band": peer}
+        )
+
     for k in range(1, bands):
-        peer = band_peer(k)
-        for ref, send, recv in (
-            (matrices_ref, mat_band_send, mat_band_recv),
-            (weights_ref, weight_band_send, weight_band_recv),
-        ):
-            whole = remote(ref.at[peer], ref.at[peer], send.at[peer], recv.at[peer], {"band": peer})
-            whole.wait_recv()
+        peer = band_peer(bands - k)
+        mat_band_all(peer).wait_recv()
+        weight_band_all(peer, parity).wait_recv()
+        twin_copy(peer, parity).start()
+    for b in range(bands):
+        twin_copy(b, 1 - parity).wait_recv()
+    code_copies.wait()
+
+    edge = (tile == 0) | (tile == tiles - 1)
+    inner = jnp.minimum(tile, tiles - 1 - tile)
+    outward = jnp.where(tile < tiles - 1 - tile, 1, -1)
+
+    def nearest(n):
+        near = ((n + 1) // 2) * (1 - 2 * lax.rem(n, 2))
+        return tile + jnp.where(n <= 2 * inner, near, (n - inner) * outward)
+
+    stages = (stage_even, stage_odd)
+
+    def stage(n, odd):
+        return pltpu.make_async_copy(
+            planes_ref.at[nearest(n)], stages[odd], local_sems.at[5 + odd]
+        )
+
+    stage(0, 0).start()
 
     def reproject(first, last):
-        def turn(n, carry):
-            source = tile + (n // 2) * (1 - 2 * (n % 2))
-
-            @pl.when((source >= 0) & (source < tiles) & (n != 1))
-            def _():
-                @pl.when(n > 0)
+        def turn(m, carry):
+            for odd in range(2):
+                n = 2 * m + odd
+                stage(n, odd).wait()
+
+                @pl.when((n + 1 < tiles) & jnp.logical_not(edge))
                 def _():
-                    arrive(source)
-
-                copies = [
-                    pltpu.make_async_copy(planes_ref.at[source], stage_x, local_sems.at[5]),
-                    pltpu.make_async_copy(codes_ref.at[source], stage_code, local_sems.at[6]),
-                ]
-                for b in range(bands):
-                    copies.append(
-                        pltpu.make_async_copy(
-                            weights_ref.at[b, source], stage_w.at[b], local_sems.at[7 + 2 * b]
-                        )
-                    )
-                    copies.append(
-                        pltpu.make_async_copy(
-                            matrices_ref.at[b, source], stage_m.at[b], local_sems.at[8 + 2 * b]
-                        )
-                    )
-                for copy in copies:
-                    copy.start()
-                for copy in copies:
-                    copy.wait()
+                    stage(n + 1, 1 - odd).start()
+
                 for r in range(cap):
                     reproject_slot(
-                        r, source * cap + r, stage_code, stage_x, stage_w, stage_m, q_ref, y_ref,
-                        wt_ref,
+                        r, cap, nearest(n), stage_code, stages[odd], weights_ref, matrices_ref,
+                        q_ref, y_ref, wt_ref,
                     )
 
+                @pl.when((n + 1 < tiles) & edge)
+                def _():
+                    plane_copy(nearest(n + 1), tile, right_send).wait_recv()
+                    stage(n + 1, 1 - odd).start()
+
             return carry
 
-        lax.fori_loop(2 * first, 2 * last, turn, 0)
+        lax.fori_loop(first, last, turn, 0)
 
     if tiles <= 8:
-        begun = 0
-        for s in range(3, tiles, 3):
-            reproject(begun, s)
-            begun = s
-            if steps < tiles:
-                forward(steps)
-                steps += 1
+        reproject(0, tiles // 4)
         for_tiles(steps, forward)
-        reproject(begun, tiles)
+        reproject(tiles // 4, tiles // 2)
     else:
         for_tiles(steps, forward)
-        reproject(0, tiles)
+        reproject(0, tiles // 2)
 
     robust_merge(y_ref, wt_ref, field_ref, u_ref, v_ref)
 
@@ -519,9 +547,9 @@
     def finish(k):
         code_copy(tile_peer(k), tile).wait_send()
         mat_copy(tile_peer(k), tile).wait_send()
-        weight_copy(tile_peer(k), tile).wait_send()
 
     for_tiles(1, finish)
+    for_same(lambda k: weight_copy(tile_peer(k), tile).wait_send())
 
     def finish_planes(shard):
         @pl.when((shard <= tile) & (tile < tiles - 1))
@@ -536,12 +564,10 @@
     for k in range(1, bands):
         peer = band_peer(k)
         x_copy(peer, band).wait_send()
-        for ref, send, recv in (
-            (matrices_ref, mat_band_send, mat_band_recv),
-            (weights_ref, weight_band_send, weight_band_recv),
-        ):
-            whole = remote(ref.at[peer], ref.at[peer], send.at[peer], recv.at[peer], {"band": peer})
-            whole.wait_send()
+        mat_band_all(peer).wait_send()
+        weight_band_all(peer, parity).wait_send()
+    for b in range(bands):
+        twin_copy(b, parity).wait_send()
 
 
 def exchange(quarters, laid, sent, meta, valid_rows, scene_order, w_in, w_hidden, w_out):
@@ -558,38 +584,37 @@
     return pl.pallas_call(
         exchange_kernel,
         in_specs=[anywhere] * 4 + [smem] * 2 + [vmem] * 6,
-        out_specs=[vmem] + [anywhere] * 4,
+        out_specs=[vmem] + [anywhere] * 2,
         out_shape=[
             jax.ShapeDtypeStruct(laid.shape[1:], F32),
             jax.ShapeDtypeStruct((tiles,) + laid.shape, BF),
-            jax.ShapeDtypeStruct((bands, tiles, scenes, lines, 128), BF),
-            jax.ShapeDtypeStruct((bands, tiles, cap) + sent.shape[1:], BF),
             jax.ShapeDtypeStruct(meta.shape, jnp.int32),
         ],
         scratch_shapes=[
+            pltpu.VMEM((bands, 2, tiles // 2, scenes, lines, 128), BF),
+            pltpu.VMEM((bands, tiles, cap) + sent.shape[1:], BF),
             pltpu.VMEM(quarters.shape, BF),
             pltpu.VMEM((scenes, lines, 128), BF),
             pltpu.VMEM((hid, bands * part), BF),
             pltpu.VMEM((layers, hid, hid), BF),
             pltpu.VMEM(laid.shape, BF),
-            pltpu.VMEM((bands, scenes, lines, 128), BF),
-            pltpu.VMEM((bands, cap) + sent.shape[1:], BF),
-            pltpu.SMEM(meta.shape[1:], jnp.int32),
+            pltpu.VMEM(laid.shape, BF),
+            pltpu.SMEM(meta.shape, jnp.int32),
             pltpu.VMEM((tiles * cap, 64, 256), F32),
             pltpu.VMEM((tiles * cap, 64, 128), F32),
             pltpu.VMEM((64, 256), F32),
             pltpu.VMEM((64, 256), F32),
             pltpu.VMEM((64, 256), F32),
             pltpu.VMEM((part, 64, 128), F32),
-            dma((7 + 2 * bands,)),
+            dma((7,)),
             dma((bands,)),
             dma((bands,)),
         ]
         + [dma((tiles,))] * 9
-        + [dma((bands,))] * 4
+        + [dma((bands,))] * 6
         + [dma((2,))] * 2,
         compiler_params=pltpu.CompilerParams(
-            collective_id=0, has_side_effects=True, vmem_limit_bytes=32 * 1024 * 1024
+            collective_id=0, has_side_effects=True, vmem_limit_bytes=40 * 1024 * 1024
         ),
     )(
         quarters, laid, sent, meta, valid_rows, scene_order, w_in, w_hidden, w_out[None, :],

time: 103 us -> 94.1 us (0.914)
  Pallas kernels: 94.5 us -> 85.6 us
    pallas_call x1, Pallas kernels: 94.5 us -> 85.6 us  [exchange(): pl.pallas_call(exchange_kernel, in_specs=[anywhere] * 4 + [smem] * 2 + [v...]
where the time goes in v5:
time: 94.1 us; the launch traced here: 93.5 us
  Pallas kernels  85.6 us (91%)
  local copies, waits for them, and re-layouts  6.47 us (7%)
    pallas_call x1, Pallas kernels, exchange(): pl.pallas_call(exchange_kernel, in_specs=[anywhere] * 4 + [smem] * 2 + [v...  85.6 us

profile of v5, /device:TPU:1, one launch (start us, length us, event | category | flops | bytes accessed | tf_op | source)
XLA Modules:
  0.0 93.5 jit_solution(13108189163514541736)
XLA Ops:
  0.0 0.0 copy-start.1
  0.0 0.0 copy-start.3
  0.0 0.0 copy-start.2
  0.0 0.0 copy-start
  0.0 0.0 copy-start.5
  0.0 0.0 copy-start.6
  0.0 0.0 copy-start.4
  0.1 0.7 broadcast_in_dim.23.w_out_raw
  0.8 0.1 eq.54
  0.9 0.8 copy.15
  1.6 0.1 eq.47
  1.7 0.2 reduce_window_sum.11
  2.0 0.2 select_reduce_fusion
  2.3 1.1 %constant_dynamic-slice_fusion = (bf16[16,4,1024]{2,1,0:T(4,128)(2,1)S(1)}, bf16[16,4,1024]{2,1,0:T(4,128)(2,1)S(1)}) fusion(bf16[16,4,4096]{2,1,0:T(4,128)(2,1)} %param.19, s32[]{:T(128)S(6)} %select_n.17, bf16[16,4,4096]{2,1,0:T(4,128)(2,1)} %param.18), kind=kLoop, calls=%fused_computation.25 | loop fusion | bytes 524292 | tf_op jit(solution)/shard_map/dynamic_slice | solution.py:658
  3.4 0.3 fusion
  3.8 1.6 %reshape.120.laid_ref = bf16[16,4,32,128]{3,2,1,0:T(8,128)(2,1)S(1)} reshape(bf16[16,4,4096]{2,1,0:T(4,128)(2,1)} %param.14) | data formatting | bytes 1048576 | tf_op jit(solution)/shard_map/reshape | solution.py:646
  5.3 1.3 %slice_bitcast_fusion.3 = (bf16[1,16,4,1024]{3,2,1,0:T(4,128)(2,1)S(1)}, bf16[1,16,4,1024]{3,2,1,0:T(4,128)(2,1)S(1)}, bf16[1,16,4,1024]{3,2,1,0:T(4,128)(2,1)S(1)}, bf16[1,16,4,1024]{3,2,1,0:T(4,128)(2,1)S(1)}) fusion(bf16[16,4,4096]{2,1,0:T(4,128)(2,1)} %param.14), kind=kLoop, calls=%fused_computation.9 | loop fusion | bytes 1048576 | tf_op jit(solution)/shard_map/stack | solution.py:647
  6.6 0.5 pad_maximum_fusion.quarters_ref
  7.1 0.0 copy-done.1
  7.1 0.0 copy-done.3
  7.1 0.0 copy-done.2
  7.2 0.0 copy-done
  7.2 0.0 copy-done.5
  7.2 0.0 copy-done.6
  7.2 0.0 copy-done.4
  7.2 85.6 %shard_map.118 = (f32[4,32,128]{2,1,0:T(8,128)S(1)}, bf16[8,16,4,32,128]{4,3,2,1,0:T(8,128)(2,1)}, s32[8,8,128]{2,1,0:T(8,128)}) custom-call(bf16[4,16,4,1024]{3,2,1,0:T(4,128)(2,1)S(1)} %pad_maximum_fusion.quarters_ref, bf16[16,4,32,128]{3,2,1,0:T(8,128)(2,1)S(1)} %reshape.120.laid_ref, bf16[72,16,128]{2,1,0:T(8,128)(2,1)S(1)} %bitcast.18, ...), custom_call_target="tpu_custom_call" | custom-call | tf_op jit(solution)/shard_map/pallas_call | solution.py:584
  92.8 0.7 copy.20
  (13 shorter events, 0.2 us)
Async XLA Ops:
  0.0 7.1 %copy-start.1 = (f32[128,128]{1,0:T(8,128)S(1)}, f32[128,128]{1,0:T(8,128)}, u32[]{:S(2)}) copy-start(f32[128,128]{1,0:T(8,128)} %constant.73.clone.v_ref) | copy-start | bytes 196612
  0.0 7.1 %copy-start.3 = (f32[64,64]{1,0:T(8,128)S(1)}, f32[64,64]{1,0:T(8,128)}, u32[]{:S(2)}) copy-start(f32[64,64]{1,0:T(8,128)} %constant.72.clone.u_ref) | copy-start | bytes 49156
  0.0 7.1 %copy-start.2 = (bf16[128,256]{1,0:T(8,128)(2,1)S(1)}, bf16[128,256]{1,0:T(8,128)(2,1)}, u32[]{:S(2)}) copy-start(bf16[128,256]{1,0:T(8,128)(2,1)} %constant.71.clone.q_ref) | copy-start | bytes 196612
  0.0 7.1 %copy-start = (bf16[2,256,256]{2,1,0:T(8,128)(2,1)S(1)}, bf16[2,256,256]{2,1,0:T(8,128)(2,1)}, u32[]{:S(2)}) copy-start(bf16[2,256,256]{2,1,0:T(8,128)(2,1)} %w_hid_raw.1) | copy-start | bytes 786436
  0.0 7.1 %copy-start.5 = (bf16[16,256]{1,0:T(8,128)(2,1)S(1)}, bf16[16,256]{1,0:T(8,128)(2,1)}, u32[]{:S(2)}) copy-start(bf16[16,256]{1,0:T(8,128)(2,1)} %w_in_raw.1) | copy-start | bytes 24580
  0.0 7.1 %copy-start.6 = (s32[16]{0:T(128)S(1)}, s32[16]{0:T(128)}, u32[]{:S(2)}) copy-start(s32[16]{0:T(128)} %order_ref.1) | copy-start | bytes 196
  0.0 7.1 %copy-start.4 = (s32[16,64]{1,0:T(8,128)S(1)}, s32[16,64]{1,0:T(8,128)}, u32[]{:S(2)}) copy-start(s32[16,64]{1,0:T(8,128)} %valid_ref.1) | copy-start | bytes 12292

commit v6 on v5

--- a/solution.py
+++ b/solution.py
@@ -92,11 +92,11 @@
             return sums[0] + h * y, sums[1] + h
 
         empty = (jnp.zeros((chunk, 256), F32), jnp.zeros((chunk, 256), F32))
-        top, bottom = lax.fori_loop(0, slots, plain, empty, unroll=4)
+        top, bottom = lax.fori_loop(0, slots, plain, empty, unroll=8)
         estimate = top / (bottom + prior_weight)
         for _ in range(HUBER_ITERS):
             top, bottom = lax.fori_loop(
-                0, slots, functools.partial(robust, estimate), empty, unroll=4
+                0, slots, functools.partial(robust, estimate), empty, unroll=8
             )
             estimate = top / (bottom + prior_weight / huber_delta)
         field_ref[here, :] = estimate
@@ -130,7 +130,7 @@
 
 
 def exchange_kernel(
-    quarters_ref,
+    granules_ref,
     laid_ref,
     sent_ref,
     meta_ref,
@@ -182,7 +182,7 @@
     halo_recv,
 ):
     tiles = planes_ref.shape[0]
-    bands = quarters_ref.shape[0]
+    bands = x_ref.shape[0]
     scenes = laid_ref.shape[0]
     cap = sent_ref.shape[0] // tiles
     tile = lax.axis_index("tile")
@@ -203,6 +203,14 @@
             return carry
 
         lax.fori_loop(first, tiles, step, 0)
+
+    edge = (tile == 0) | (tile == tiles - 1)
+    inner = jnp.minimum(tile, tiles - 1 - tile)
+    outward = jnp.where(tile < tiles - 1 - tile, 1, -1)
+
+    def nearest(n):
+        near = ((n + 1) // 2) * (1 - 2 * lax.rem(n, 2))
+        return tile + jnp.where(n <= 2 * inner, near, (n - inner) * outward)
 
     barrier = pltpu.get_barrier_semaphore()
     for_tiles(
@@ -225,9 +233,14 @@
             device_id_type=MESH,
         )
 
+    width = x_ref.shape[3]
+
+    def quarter(b):
+        return granules_ref.at[:, :, pl.ds(pl.multiple_of(b * width, width), width)]
+
     def x_copy(peer, source):
         return remote(
-            quarters_ref.at[peer], x_ref.at[source], x_send.at[peer], x_recv.at[source],
+            quarter(peer), x_ref.at[source], x_send.at[peer], x_recv.at[source],
             {"band": peer},
         )
 
@@ -281,7 +294,7 @@
 
     for k in range(1, bands):
         x_copy(band_peer(k), band).start()
-    x_local = pltpu.make_async_copy(quarters_ref.at[band], x_ref.at[band], local_sems.at[0])
+    x_local = pltpu.make_async_copy(quarter(band), x_ref.at[band], local_sems.at[0])
     x_local.start()
 
     @pl.when(tile < tiles - 1)
@@ -344,18 +357,15 @@
         own_ref[scene] = (jnp.concatenate(pieces, axis=0) * valid * recency).astype(BF)
         return carry
 
-    def share_matrices():
-        mat_local.wait()
-        for k in range(1, bands):
-            mat_band_copy(tile, band_peer(k), band).start()
-
-        def share(k):
-            source = tile_source(k)
+    def share_matrices(first, last):
+        def share(n, carry):
+            source = nearest(n)
             mat_copy(tile, source).wait_recv()
             for j in range(1, bands):
                 mat_band_copy(source, band_peer(j), band).start()
-
-        for_tiles(1, share)
+            return carry
+
+        lax.fori_loop(first, last, share, 0)
 
     w_in_ref[...] = (w_in_raw[...].astype(F32) * 0.5).T.astype(BF)
     for layer in range(w_hid_raw.shape[0]):
@@ -365,13 +375,16 @@
         x_copy(source, source).wait_recv()
     x_local.wait()
     steps = 1
-    for first, last in ((0, 3), (3, 7), (7, 13), (13, 16)):
+    for part in range(4):
         if steps < min(4, tiles):
             forward(steps)
             steps += 1
-        if first == 7:
-            share_matrices()
-        lax.fori_loop(first * scenes // 16, last * scenes // 16, network, 0)
+        if part == 2:
+            mat_local.wait()
+            for k in range(1, bands):
+                mat_band_copy(tile, band_peer(k), band).start()
+            share_matrices(1, tiles // 2)
+        lax.fori_loop(part * scenes // 4, (part + 1) * scenes // 4, network, 0, unroll=2)
 
     weight_local = pltpu.make_async_copy(
         own_ref, weights_ref.at[band, parity, tile // 2], local_sems.at[4]
@@ -390,16 +403,17 @@
     for k in range(1, bands):
         weight_band_copy(tile, band_peer(k), band).start()
 
-    def share_weights(k):
-        source = tile_source(k)
-        weight_copy(tile, source).wait_recv()
-        for j in range(1, bands):
-            weight_band_copy(source, band_peer(j), band).start()
-
-    if steps < tiles:
-        forward(steps)
-        steps += 1
-    for_same(share_weights)
+    def share_weights(n):
+        source = nearest(n)
+
+        @pl.when(lax.rem(source + tile, 2) == 0)
+        def _():
+            weight_copy(tile, source).wait_recv()
+            for j in range(1, bands):
+                weight_band_copy(source, band_peer(j), band).start()
+
+    share_matrices(tiles // 2, tiles)
+    for_tiles(1, share_weights)
     twin_copy(band, parity).start()
     if steps < tiles:
         forward(steps)
@@ -430,14 +444,6 @@
     for b in range(bands):
         twin_copy(b, 1 - parity).wait_recv()
     code_copies.wait()
-
-    edge = (tile == 0) | (tile == tiles - 1)
-    inner = jnp.minimum(tile, tiles - 1 - tile)
-    outward = jnp.where(tile < tiles - 1 - tile, 1, -1)
-
-    def nearest(n):
-        near = ((n + 1) // 2) * (1 - 2 * lax.rem(n, 2))
-        return tile + jnp.where(n <= 2 * inner, near, (n - inner) * outward)
 
     stages = (stage_even, stage_odd)
 
@@ -570,8 +576,9 @@
         twin_copy(b, parity).wait_send()
 
 
-def exchange(quarters, laid, sent, meta, valid_rows, scene_order, w_in, w_hidden, w_out):
-    bands, scenes, part, width = quarters.shape
+def exchange(granules, bands, laid, sent, meta, valid_rows, scene_order, w_in, w_hidden, w_out):
+    scenes, part, pixels = granules.shape
+    width = pixels // bands
     tiles = meta.shape[0]
     cap = sent.shape[0] // tiles
     hid = w_in.shape[1]
@@ -593,7 +600,7 @@
         scratch_shapes=[
             pltpu.VMEM((bands, 2, tiles // 2, scenes, lines, 128), BF),
             pltpu.VMEM((bands, tiles, cap) + sent.shape[1:], BF),
-            pltpu.VMEM(quarters.shape, BF),
+            pltpu.VMEM((bands, scenes, part, width), BF),
             pltpu.VMEM((scenes, lines, 128), BF),
             pltpu.VMEM((hid, bands * part), BF),
             pltpu.VMEM((layers, hid, hid), BF),
@@ -617,7 +624,7 @@
             collective_id=0, has_side_effects=True, vmem_limit_bytes=40 * 1024 * 1024
         ),
     )(
-        quarters, laid, sent, meta, valid_rows, scene_order, w_in, w_hidden, w_out[None, :],
+        granules, laid, sent, meta, valid_rows, scene_order, w_in, w_hidden, w_out[None, :],
         *order_matrices(),
     )[0]
 
@@ -644,7 +651,6 @@
     part = pixel_count // band_count
 
     laid = granules.reshape(scenes, group_bands, pixel_count // 128, 128)
-    quarters = jnp.stack([granules[:, :, b * part : (b + 1) * part] for b in range(band_count)])
     flat_dest = intersections.reshape(entry_count)
     is_dest = flat_dest[None, :] == jnp.arange(tile_count, dtype=jnp.int32)[:, None]
     rank = jnp.cumsum(is_dest.astype(jnp.int32), 1) - 1
@@ -663,7 +669,7 @@
     sent = jnp.dot(pick, both, preferred_element_type=F32).astype(BF)
     sent = sent.reshape(tile_count * cap, 2 * part // 128, 128)
     field = exchange(
-        quarters, laid, sent, meta, valid_rows, scene_order, w_in, w_hidden, w_out
+        granules, band_count, laid, sent, meta, valid_rows, scene_order, w_in, w_hidden, w_out
     )
     return field.reshape(group_bands, pixel_count)
 

time: 94.1 us -> 106 us (1.13); the launches traced: 93.5 us -> 104 us
  Pallas kernels: 85.6 us -> 91.8 us
  local copies, waits for them, and re-layouts: 6.47 us -> 11.6 us
    unnamed x17 -> x19, local copies, waits for them, and re-layouts: 1.51 us -> 7.95 us
    pallas_call x1, Pallas kernels: 85.6 us -> 91.8 us  [exchange(): pl.pallas_call(exchange_kernel, in_specs=[anywhere] * 4 + [smem] * 2 + [v...]
    another operation x1 -> x0, local copies, waits for them, and re-layouts: 1.29 us -> none  [per_device(): jnp.stack([granules[:, :, b * part:(b + 1) * part] for b in range(band_co...]
where the time goes in v6:
time: 106 us; the launch traced here: 104 us
  Pallas kernels  91.8 us (87%)
  local copies, waits for them, and re-layouts  11.6 us (11%)
    pallas_call x1, Pallas kernels, exchange(): pl.pallas_call(exchange_kernel, in_specs=[anywhere] * 4 + [smem] * 2 + [v...  91.8 us
    unnamed x19, local copies, waits for them, and re-layouts  7.95 us

profile of v6, /device:TPU:1, one launch (start us, length us, event | category | flops | bytes accessed | tf_op | source)
XLA Modules:
  0.0 104.2 jit_solution(16411108417007933466)
XLA Ops:
  0.0 0.7 broadcast_in_dim.23.w_out_raw
  0.7 0.1 eq.54
  0.7 0.8 copy.15
  1.5 0.1 eq.47
  1.6 0.2 reduce_window_sum.11
  1.8 0.2 select_reduce_fusion
  2.2 1.1 %constant_dynamic-slice_fusion = (bf16[16,4,1024]{2,1,0:T(4,128)(2,1)S(1)}, bf16[16,4,1024]{2,1,0:T(4,128)(2,1)S(1)}) fusion(bf16[16,4,4096]{2,1,0:T(4,128)(2,1)} %param.19, s32[]{:T(128)S(6)} %select_n.17, bf16[16,4,4096]{2,1,0:T(4,128)(2,1)} %param.18), kind=kLoop, calls=%fused_computation.20 | loop fusion | bytes 524292 | tf_op jit(solution)/shard_map/dynamic_slice | solution.py:664
  3.3 0.3 fusion
  3.6 1.6 %reshape.120.laid_ref = bf16[16,4,32,128]{3,2,1,0:T(8,128)(2,1)S(1)} reshape(bf16[16,4,4096]{2,1,0:T(4,128)(2,1)} %granules_ref.1) | data formatting | bytes 1048576 | tf_op jit(solution)/shard_map/reshape | solution.py:653
  5.2 0.0 copy-start
  5.2 1.0 copy-done
  6.3 0.0 copy-start.1
  6.3 0.9 copy-done.1
  7.2 0.0 copy-start.2
  7.2 0.8 copy-done.2
  8.1 0.0 copy-start.3
  8.1 0.8 copy-done.3
  8.9 0.0 copy-start.4
  8.9 0.8 copy-done.4
  9.7 0.0 copy-start.5
  9.7 0.7 copy-done.5
  10.4 0.0 copy-start.6
  10.4 0.7 copy-done.6
  11.1 0.0 copy-start.7
  11.1 0.7 copy-done.7
  11.7 91.8 %shard_map.118 = (f32[4,32,128]{2,1,0:T(8,128)S(1)}, bf16[8,16,4,32,128]{4,3,2,1,0:T(8,128)(2,1)}, s32[8,8,128]{2,1,0:T(8,128)}) custom-call(bf16[16,4,4096]{2,1,0:T(4,128)(2,1)S(1)} %copy-done, bf16[16,4,32,128]{3,2,1,0:T(8,128)(2,1)S(1)} %reshape.120.laid_ref, bf16[72,16,128]{2,1,0:T(8,128)(2,1)S(1)} %bitcast.10, s32[8,8,128]{2,1,0:T(8,128)S(1)} %scatter.4.meta_ref, ...), custom_call_target="tpu_custom_call" | custom-call | tf_op jit(solution)/shard_map/pallas_call | solution.py:591
  103.5 0.7 copy.20
  (13 shorter events, 0.2 us)
Async XLA Ops:
  5.2 1.0 %copy-start = (bf16[16,4,4096]{2,1,0:T(4,128)(2,1)S(1)}, bf16[16,4,4096]{2,1,0:T(4,128)(2,1)}, u32[]{:S(2)}) copy-start(bf16[16,4,4096]{2,1,0:T(4,128)(2,1)} %granules_ref.1) | copy-start | bytes 1572868
  6.3 0.9 copy-start.1
  7.2 0.8 copy-start.2
  8.1 0.8 copy-start.3
  8.9 0.8 copy-start.4
  9.7 0.7 copy-start.5
  10.4 0.7 copy-start.6
  11.1 0.7 copy-start.7

commit v7 on v6

--- a/solution.py
+++ b/solution.py
@@ -92,11 +92,11 @@
             return sums[0] + h * y, sums[1] + h
 
         empty = (jnp.zeros((chunk, 256), F32), jnp.zeros((chunk, 256), F32))
-        top, bottom = lax.fori_loop(0, slots, plain, empty, unroll=8)
+        top, bottom = lax.fori_loop(0, slots, plain, empty, unroll=4)
         estimate = top / (bottom + prior_weight)
         for _ in range(HUBER_ITERS):
             top, bottom = lax.fori_loop(
-                0, slots, functools.partial(robust, estimate), empty, unroll=8
+                0, slots, functools.partial(robust, estimate), empty, unroll=4
             )
             estimate = top / (bottom + prior_weight / huber_delta)
         field_ref[here, :] = estimate
@@ -130,7 +130,7 @@
 
 
 def exchange_kernel(
-    granules_ref,
+    quarters_ref,
     laid_ref,
     sent_ref,
     meta_ref,
@@ -233,14 +233,9 @@
             device_id_type=MESH,
         )
 
-    width = x_ref.shape[3]
-
-    def quarter(b):
-        return granules_ref.at[:, :, pl.ds(pl.multiple_of(b * width, width), width)]
-
     def x_copy(peer, source):
         return remote(
-            quarter(peer), x_ref.at[source], x_send.at[peer], x_recv.at[source],
+            quarters_ref.at[peer], x_ref.at[source], x_send.at[peer], x_recv.at[source],
             {"band": peer},
         )
 
@@ -294,7 +289,7 @@
 
     for k in range(1, bands):
         x_copy(band_peer(k), band).start()
-    x_local = pltpu.make_async_copy(quarter(band), x_ref.at[band], local_sems.at[0])
+    x_local = pltpu.make_async_copy(quarters_ref.at[band], x_ref.at[band], local_sems.at[0])
     x_local.start()
 
     @pl.when(tile < tiles - 1)
@@ -384,7 +379,7 @@
             for k in range(1, bands):
                 mat_band_copy(tile, band_peer(k), band).start()
             share_matrices(1, tiles // 2)
-        lax.fori_loop(part * scenes // 4, (part + 1) * scenes // 4, network, 0, unroll=2)
+        lax.fori_loop(part * scenes // 4, (part + 1) * scenes // 4, network, 0)
 
     weight_local = pltpu.make_async_copy(
         own_ref, weights_ref.at[band, parity, tile // 2], local_sems.at[4]
@@ -576,9 +571,8 @@
         twin_copy(b, parity).wait_send()
 
 
-def exchange(granules, bands, laid, sent, meta, valid_rows, scene_order, w_in, w_hidden, w_out):
-    scenes, part, pixels = granules.shape
-    width = pixels // bands
+def exchange(quarters, laid, sent, meta, valid_rows, scene_order, w_in, w_hidden, w_out):
+    bands, scenes, part, width = quarters.shape
     tiles = meta.shape[0]
     cap = sent.shape[0] // tiles
     hid = w_in.shape[1]
@@ -624,7 +618,7 @@
             collective_id=0, has_side_effects=True, vmem_limit_bytes=40 * 1024 * 1024
         ),
     )(
-        granules, laid, sent, meta, valid_rows, scene_order, w_in, w_hidden, w_out[None, :],
+        quarters, laid, sent, meta, valid_rows, scene_order, w_in, w_hidden, w_out[None, :],
         *order_matrices(),
     )[0]
 
@@ -651,6 +645,8 @@
     part = pixel_count // band_count
 
     laid = granules.reshape(scenes, group_bands, pixel_count // 128, 128)
+    quarters = jnp.stack([granules[:, :, b * part : (b + 1) * part] for b in range(band_count)])
+
     flat_dest = intersections.reshape(entry_count)
     is_dest = flat_dest[None, :] == jnp.arange(tile_count, dtype=jnp.int32)[:, None]
     rank = jnp.cumsum(is_dest.astype(jnp.int32), 1) - 1
@@ -669,7 +665,7 @@
     sent = jnp.dot(pick, both, preferred_element_type=F32).astype(BF)
     sent = sent.reshape(tile_count * cap, 2 * part // 128, 128)
     field = exchange(
-        granules, band_count, laid, sent, meta, valid_rows, scene_order, w_in, w_hidden, w_out
+        quarters, laid, sent, meta, valid_rows, scene_order, w_in, w_hidden, w_out
     )
     return field.reshape(group_bands, pixel_count)
 

time: 106 us -> 102 us (0.962)
  local copies, waits for them, and re-layouts: 11.6 us -> 6.47 us
  Pallas kernels: 91.8 us -> 93.2 us
    unnamed x19 -> x17, local copies, waits for them, and re-layouts: 7.95 us -> 1.51 us
    pallas_call x1, Pallas kernels: 91.8 us -> 93.2 us  [exchange(): pl.pallas_call(exchange_kernel, in_specs=[anywhere] * 4 + [smem] * 2 + [v...]
    another operation x0 -> x1, local copies, waits for them, and re-layouts: none -> 1.29 us  [per_device(): jnp.stack([granules[:, :, b * part:(b + 1) * part] for b in range(band_co...]
where the time goes in v7:
time: 102 us; the launch traced here: 101 us
  Pallas kernels  93.2 us (91%)
  local copies, waits for them, and re-layouts  6.47 us (6%)
    pallas_call x1, Pallas kernels, exchange(): pl.pallas_call(exchange_kernel, in_specs=[anywhere] * 4 + [smem] * 2 + [v...  93.2 us

profile of v7, /device:TPU:1, one launch (start us, length us, event | category | flops | bytes accessed | tf_op | source)
XLA Modules:
  0.0 101.1 jit_solution(3788291658019137069)
XLA Ops:
  0.0 0.0 copy-start.1
  0.0 0.0 copy-start.3
  0.0 0.0 copy-start.2
  0.0 0.0 copy-start
  0.0 0.0 copy-start.5
  0.0 0.0 copy-start.6
  0.0 0.0 copy-start.4
  0.1 0.7 broadcast_in_dim.23.w_out_raw
  0.8 0.1 eq.54
  0.9 0.8 copy.15
  1.6 0.1 eq.47
  1.7 0.2 reduce_window_sum.11
  2.0 0.2 select_reduce_fusion
  2.3 1.1 %constant_dynamic-slice_fusion = (bf16[16,4,1024]{2,1,0:T(4,128)(2,1)S(1)}, bf16[16,4,1024]{2,1,0:T(4,128)(2,1)S(1)}) fusion(bf16[16,4,4096]{2,1,0:T(4,128)(2,1)} %param.19, s32[]{:T(128)S(6)} %select_n.17, bf16[16,4,4096]{2,1,0:T(4,128)(2,1)} %param.18), kind=kLoop, calls=%fused_computation.25 | loop fusion | bytes 524292 | tf_op jit(solution)/shard_map/dynamic_slice | solution.py:660
  3.4 0.3 fusion
  3.8 1.6 %reshape.120.laid_ref = bf16[16,4,32,128]{3,2,1,0:T(8,128)(2,1)S(1)} reshape(bf16[16,4,4096]{2,1,0:T(4,128)(2,1)} %param.14) | data formatting | bytes 1048576 | tf_op jit(solution)/shard_map/reshape | solution.py:647
  5.3 1.3 %slice_bitcast_fusion.3 = (bf16[1,16,4,1024]{3,2,1,0:T(4,128)(2,1)S(1)}, bf16[1,16,4,1024]{3,2,1,0:T(4,128)(2,1)S(1)}, bf16[1,16,4,1024]{3,2,1,0:T(4,128)(2,1)S(1)}, bf16[1,16,4,1024]{3,2,1,0:T(4,128)(2,1)S(1)}) fusion(bf16[16,4,4096]{2,1,0:T(4,128)(2,1)} %param.14), kind=kLoop, calls=%fused_computation.9 | loop fusion | bytes 1048576 | tf_op jit(solution)/shard_map/stack | solution.py:648
  6.6 0.5 pad_maximum_fusion.quarters_ref
  7.1 0.0 copy-done.1
  7.1 0.0 copy-done.3
  7.1 0.0 copy-done.2
  7.2 0.0 copy-done
  7.2 0.0 copy-done.5
  7.2 0.0 copy-done.6
  7.2 0.0 copy-done.4
  7.2 93.2 %shard_map.118 = (f32[4,32,128]{2,1,0:T(8,128)S(1)}, bf16[8,16,4,32,128]{4,3,2,1,0:T(8,128)(2,1)}, s32[8,8,128]{2,1,0:T(8,128)}) custom-call(bf16[4,16,4,1024]{3,2,1,0:T(4,128)(2,1)S(1)} %pad_maximum_fusion.quarters_ref, bf16[16,4,32,128]{3,2,1,0:T(8,128)(2,1)S(1)} %reshape.120.laid_ref, bf16[72,16,128]{2,1,0:T(8,128)(2,1)S(1)} %bitcast.18, ...), custom_call_target="tpu_custom_call" | custom-call | tf_op jit(solution)/shard_map/pallas_call | solution.py:585
  100.4 0.7 copy.20
  (13 shorter events, 0.2 us)
Async XLA Ops:
  0.0 7.1 %copy-start.1 = (f32[128,128]{1,0:T(8,128)S(1)}, f32[128,128]{1,0:T(8,128)}, u32[]{:S(2)}) copy-start(f32[128,128]{1,0:T(8,128)} %constant.73.clone.v_ref) | copy-start | bytes 196612
  0.0 7.1 %copy-start.3 = (f32[64,64]{1,0:T(8,128)S(1)}, f32[64,64]{1,0:T(8,128)}, u32[]{:S(2)}) copy-start(f32[64,64]{1,0:T(8,128)} %constant.72.clone.u_ref) | copy-start | bytes 49156
  0.0 7.1 %copy-start.2 = (bf16[128,256]{1,0:T(8,128)(2,1)S(1)}, bf16[128,256]{1,0:T(8,128)(2,1)}, u32[]{:S(2)}) copy-start(bf16[128,256]{1,0:T(8,128)(2,1)} %constant.71.clone.q_ref) | copy-start | bytes 196612
  0.0 7.1 %copy-start = (bf16[2,256,256]{2,1,0:T(8,128)(2,1)S(1)}, bf16[2,256,256]{2,1,0:T(8,128)(2,1)}, u32[]{:S(2)}) copy-start(bf16[2,256,256]{2,1,0:T(8,128)(2,1)} %w_hid_raw.1) | copy-start | bytes 786436
  0.0 7.1 %copy-start.5 = (bf16[16,256]{1,0:T(8,128)(2,1)S(1)}, bf16[16,256]{1,0:T(8,128)(2,1)}, u32[]{:S(2)}) copy-start(bf16[16,256]{1,0:T(8,128)(2,1)} %w_in_raw.1) | copy-start | bytes 24580
  0.0 7.1 %copy-start.6 = (s32[16]{0:T(128)S(1)}, s32[16]{0:T(128)}, u32[]{:S(2)}) copy-start(s32[16]{0:T(128)} %order_ref.1) | copy-start | bytes 196
  0.0 7.1 %copy-start.4 = (s32[16,64]{1,0:T(8,128)S(1)}, s32[16,64]{1,0:T(8,128)}, u32[]{:S(2)}) copy-start(s32[16,64]{1,0:T(8,128)} %valid_ref.1) | copy-start | bytes 12292
